TPU v7x, 128 devices: a whole 4x4x4 slice. The times are simulated.
128 devices in a mesh: region: 16 (over y, z), loop: 8 (over x, core).
Axes of the slice: x: 4, y: 4, z: 4, core: 2. Of those that a mesh axis runs over, the one named last changes fastest.
Arguments:
- tokens: bfloat16 [65536, 256], P(('region', 'loop')), may hold values from -6 to 6
- dest: int32 [65536, 1], P(('region', 'loop')), may hold values from 0 to 127; in each aligned block of 512 rows (0 to 511, 512 to 1023, ...) at most 8 rows name the same one
- norm1_gain: float32 [256], replicated, may hold values from 0.1 to 1.9
- w_qkv: bfloat16 [256, 768], replicated, may hold values from -0.8125 to 0.8125
- w_out: bfloat16 [256, 256], replicated, may hold values from -0.375 to 0.375
- norm2_gain: float32 [256], replicated, may hold values from 0.1 to 1.9
- w_hidden: bfloat16 [256, 1024], replicated, may hold values from -0.375 to 0.375
- w_back: bfloat16 [1024, 256], replicated, may hold values from -0.1875 to 0.1875
Outputs:
- updated: bfloat16 [65536, 256], P(('region', 'loop'))
Inputs may be any that keep to these rules, and one draw needn't show every extreme that they name: `dest`: among the grains of one device, at most 8 have the same owner; in every draw some device sends exactly 8 grains to one owner. Every device is the owner of some grain.
All inputs are finite; a program needn't handle non-finite values.
Results may differ from a plain program's by a relative error of at most 0.011.
Values may be sent and summed in bfloat16 or wider, within the bound.
A program may use at most 128 MiB of HBM per device.

v0:
```python
import jax
import jax.numpy as jnp
from jax import lax
from jax.sharding import PartitionSpec as P

D = 256
HEADS = 8


def layer_norm(values, gain):
    mean = jnp.mean(values, axis=-1, keepdims=True)
    centered = values - mean
    variance = jnp.mean(centered * centered, axis=-1, keepdims=True)
    return centered * lax.rsqrt(variance + 1e-05) * gain


def attend(state, queries, keys, values, flags):
    piece_rows = keys.shape[0]
    block = 512
    count = piece_rows // block
    key_blocks = keys.reshape(count, block, HEADS, -1)
    value_blocks = values.reshape(count, block, HEADS, -1)
    flag_blocks = flags.reshape(count, block)
    scale = 1.0 / key_blocks.shape[3] ** 0.5

    def step(carry, block_in):
        running_top, running_total, accum = carry
        key_block, value_block, flag_block = block_in
        scores = (
            jnp.einsum("qhe,khe->qhk", queries, key_block, preferred_element_type=jnp.float32)
            * scale
        )
        alive = flag_block[None, None, :] > 0
        masked = jnp.where(alive, scores, -1e30)
        new_top = jnp.maximum(running_top, jnp.max(masked, axis=2))
        factor = jnp.exp(running_top - new_top)
        weights = jnp.where(alive, jnp.exp(masked - new_top[:, :, None]), 0.0)
        new_total = running_total * factor + jnp.sum(weights, axis=2)
        new_accum = accum * factor[:, :, None] + jnp.einsum(
            "qhk,khe->qhe",
            weights.astype(jnp.bfloat16),
            value_block,
            preferred_element_type=jnp.float32,
        )
        return ((new_top, new_total, new_accum), None)

    state, unused = lax.scan(step, state, (key_blocks, value_blocks, flag_blocks))
    return state


def local(tokens, dest, norm1_gain, w_qkv, w_out, norm2_gain, w_hidden, w_back):
    row_count = tokens.shape[0]
    model_width = tokens.shape[1]
    region_count = lax.axis_size("region")
    loop_count = lax.axis_size("loop")
    dev_count = region_count * loop_count
    capacity = 2 * row_count // dev_count
    slot_count = dev_count * capacity
    target = dest[:, 0]
    onehot = (target[:, None] == jnp.arange(dev_count, dtype=jnp.int32)[None, :]).astype(
        jnp.bfloat16
    )
    row_index = jnp.arange(row_count, dtype=jnp.int32)
    lower = (row_index[:, None] >= row_index[None, :]).astype(jnp.bfloat16)
    before = jnp.dot(lower, onehot, preferred_element_type=jnp.float32)
    rank = jnp.sum(before * onehot.astype(jnp.float32), axis=1).astype(jnp.int32) - 1
    position = target * capacity + rank
    outgoing = jnp.zeros((slot_count, model_width), jnp.bfloat16).at[position].set(tokens)
    out_flags = (
        jnp.zeros((slot_count,), jnp.bfloat16)
        .at[position]
        .set(jnp.ones((row_count,), jnp.bfloat16))
    )
    moved, moved_flags = (
        lax.all_to_all(
            outgoing.reshape(dev_count, capacity, model_width),
            ("region", "loop"),
            split_axis=0,
            concat_axis=0,
            tiled=True,
        ),
        lax.all_to_all(
            out_flags.reshape(dev_count, capacity),
            ("region", "loop"),
            split_axis=0,
            concat_axis=0,
            tiled=True,
        ),
    )
    received = moved.reshape(slot_count, model_width)
    flags = moved_flags.reshape(slot_count)
    flat = received.astype(jnp.float32)
    normed = layer_norm(flat, norm1_gain).astype(jnp.bfloat16)
    initial = (
        jnp.full((slot_count, HEADS), -1e30, jnp.float32),
        jnp.zeros((slot_count, HEADS), jnp.float32),
        jnp.zeros((slot_count, HEADS, model_width // HEADS), jnp.float32),
    )
    projected = jnp.dot(normed, w_qkv, preferred_element_type=jnp.float32).astype(jnp.bfloat16)
    queries = projected[:, :D].reshape(slot_count, HEADS, -1)
    key_piece = lax.all_gather(projected[:, D : 2 * D], "loop", axis=0, tiled=True)
    value_piece = lax.all_gather(projected[:, 2 * D :], "loop", axis=0, tiled=True)
    flag_piece = lax.all_gather(flags, "loop", axis=0, tiled=True)
    state = attend(initial, queries, key_piece, value_piece, flag_piece)
    running_top, running_total, accum = state
    attended = (
        (accum / running_total[:, :, None]).reshape(slot_count, model_width).astype(jnp.bfloat16)
    )
    mixed = flat + jnp.dot(attended, w_out, preferred_element_type=jnp.float32)
    normed2 = layer_norm(mixed, norm2_gain).astype(jnp.bfloat16)
    hidden = jax.nn.gelu(
        jnp.dot(normed2, w_hidden, preferred_element_type=jnp.float32), approximate=False
    ).astype(jnp.bfloat16)
    result = (mixed + jnp.dot(hidden, w_back, preferred_element_type=jnp.float32)).astype(
        jnp.bfloat16
    )
    returned = lax.all_to_all(
        result.reshape(dev_count, capacity, model_width),
        ("region", "loop"),
        split_axis=0,
        concat_axis=0,
        tiled=True,
    )
    returned = returned.reshape(slot_count, model_width)
    return returned[position]


def solution(mesh):
    return jax.shard_map(
        local,
        mesh=mesh,
        in_specs=(
            P(("region", "loop"), None),
            P(("region", "loop"), None),
            P(),
            P(),
            P(),
            P(),
            P(),
            P(),
        ),
        out_specs=P(("region", "loop"), None),
        check_vma=False,
    )
```

profile of v0, /device:TPU:1, one launch (start us, length us, event | category | flops | bytes accessed | tf_op | source)
XLA Modules:
  0.0 543.9 jit_solution(17457151478117806444)
XLA Ops:
  11.2 25.0 %all_to_all.20 = bf16[128,8,256]{2,1,0:T(8,128)(2,1)S(1)} all-to-all(bf16[128,8,256]{2,1,0:T(8,128)(2,1)S(1)} %bitcast.87), channel_id=1, replica_groups=mesh['region'=16,'loop'=8] {'region','loop'}, dimensions={0} | all-to-all | bytes 1048576 | tf_op jit(solution)/shard_map/all_to_all | solution.py:75
  50.0 9.7 %all-to-all-done.1 = bf16[128,1,8]{2,1,0:T(2,128)(2,1)S(1)} async-done(((bf16[128,1,8]{2,1,0:T(2,128)(2,1)}), bf16[128,1,8]{2,1,0:T(2,128)(2,1)S(1)}, u32[]{:S(2)}, u32[]{:S(2)}) %all-to-all-start.1) | async-done | bytes 2080 | tf_op jit(solution)/shard_map/all_to_all | solution.py:82
  60.0 12.1 %all_gather.9 = bf16[8192]{0:T(1024)(128)(2,1)S(1)} all-gather(bf16[1024]{0:T(1024)(128)(2,1)S(1)} %reshape.107), channel_id=1, replica_groups=mesh['region'=16,'loop'=8] {'loop'}, dimensions={0}, use_global_device_ids=true | all-gather | bytes 18432 | tf_op jit(solution)/shard_map/all_gather | solution.py:103
  80.5 23.0 %all-gather.5.cloned.1.call-done = bf16[8192,256]{0,1:T(8,128)(2,1)} async-done(((bf16[1024,256]{0,1:T(8,128)(2,1)}), bf16[8192,256]{0,1:T(8,128)(2,1)}) %all-gather.5.cloned.1.call-update) | async-done | bytes 4194320 | tf_op jit(solution)/shard_map/all_gather | solution.py:102
  111.9 388.9 %while.15 = (s32[]{:T(128)}, f32[1024,8]{0,1:T(8,128)S(1)}, f32[1024,8]{0,1:T(8,128)S(1)}, f32[1024,8,32]{0,2,1:T(8,128)S(1)}, bf16[16,512]{1,0:T(8,128)(2,1)S(1...) while((s32[]{:T(128)}, f32[1024,8]{0,1:T(8,128)S(1)}, ...), condition=%wide.region_8.9_spmd.clone, body=%wide.region_5.8_spmd.clone.sunk | while | flops 592225792 | bytes 121115280 | solution.py:47
  112.2 8.8 %bitcast_reduce_fusion.2 = (f32[1024,8]{0,1:T(8,128)S(1)}, f32[8,512,1024]{2,1,0:T(8,128)}) fusion(pred[512]{0:T(512)(128)(4,1)S(1)} %compare_reduce_fusion.2, bf16[1024,8,32]{0,2,1:T(8,128)(2,1)S(1)} %get-tuple-element.209, bf16[16,512,8,32]{1,3,2,0:T(8,128)(2,1)} %get-tuple-element.208, s32[]{:T(128)} %get-tuple-element.193), kind=kOutput, calls=%fused_computation.4.clone.1 | convolution fusion | flops 281010176 | bytes 17597440 | tf_op jit(solution)/shard_map/while/body/eval_jaxpr/qhe,khe->qhk/dot_general | solution.py:30
  121.0 8.5 %fusion.118 = f32[1024,8]{0,1:T(8,128)S(1)} fusion(f32[8,512,1024]{2,1,0:T(8,128)} %get-tuple-element.180, f32[1024,8]{0,1:T(8,128)S(1)} %select_maximum_fusion.2, pred[512]{0:T(512)(128)(4,1)S(1)} %compare_reduce_fusion.2), kind=kLoop, calls=%fused_computation.9.clone.1 | loop fusion | flops 20963328 | bytes 16843264 | tf_op jit(solution)/shard_map/while/body/eval_jaxpr/reduce_sum | solution.py:38
  136.4 8.8 %bitcast_reduce_fusion.2 = (f32[1024,8]{0,1:T(8,128)S(1)}, f32[8,512,1024]{2,1,0:T(8,128)}) fusion(pred[512]{0:T(512)(128)(4,1)S(1)} %compare_reduce_fusion.2, bf16[1024,8,32]{0,2,1:T(8,128)(2,1)S(1)} %get-tuple-element.209, bf16[16,512,8,32]{1,3,2,0:T(8,128)(2,1)} %get-tuple-element.208, s32[]{:T(128)} %get-tuple-element.193), kind=kOutput, calls=%fused_computation.4.clone.1 | convolution fusion | flops 281010176 | bytes 17597440 | tf_op jit(solution)/shard_map/while/body/eval_jaxpr/qhe,khe->qhk/dot_general | solution.py:30
  145.2 8.5 %fusion.118 = f32[1024,8]{0,1:T(8,128)S(1)} fusion(f32[8,512,1024]{2,1,0:T(8,128)} %get-tuple-element.180, f32[1024,8]{0,1:T(8,128)S(1)} %select_maximum_fusion.2, pred[512]{0:T(512)(128)(4,1)S(1)} %compare_reduce_fusion.2), kind=kLoop, calls=%fused_computation.9.clone.1 | loop fusion | flops 20963328 | bytes 16843264 | tf_op jit(solution)/shard_map/while/body/eval_jaxpr/reduce_sum | solution.py:38
  155.8 4.8 fusion.120
  160.7 8.8 %bitcast_reduce_fusion.2 = (f32[1024,8]{0,1:T(8,128)S(1)}, f32[8,512,1024]{2,1,0:T(8,128)}) fusion(pred[512]{0:T(512)(128)(4,1)S(1)} %compare_reduce_fusion.2, bf16[1024,8,32]{0,2,1:T(8,128)(2,1)S(1)} %get-tuple-element.209, bf16[16,512,8,32]{1,3,2,0:T(8,128)(2,1)} %get-tuple-element.208, s32[]{:T(128)} %get-tuple-element.193), kind=kOutput, calls=%fused_computation.4.clone.1 | convolution fusion | flops 281010176 | bytes 17597440 | tf_op jit(solution)/shard_map/while/body/eval_jaxpr/qhe,khe->qhk/dot_general | solution.py:30
  169.5 8.5 %fusion.118 = f32[1024,8]{0,1:T(8,128)S(1)} fusion(f32[8,512,1024]{2,1,0:T(8,128)} %get-tuple-element.180, f32[1024,8]{0,1:T(8,128)S(1)} %select_maximum_fusion.2, pred[512]{0:T(512)(128)(4,1)S(1)} %compare_reduce_fusion.2), kind=kLoop, calls=%fused_computation.9.clone.1 | loop fusion | flops 20963328 | bytes 16843264 | tf_op jit(solution)/shard_map/while/body/eval_jaxpr/reduce_sum | solution.py:38
  180.1 4.8 fusion.120
  185.0 8.8 %bitcast_reduce_fusion.2 = (f32[1024,8]{0,1:T(8,128)S(1)}, f32[8,512,1024]{2,1,0:T(8,128)}) fusion(pred[512]{0:T(512)(128)(4,1)S(1)} %compare_reduce_fusion.2, bf16[1024,8,32]{0,2,1:T(8,128)(2,1)S(1)} %get-tuple-element.209, bf16[16,512,8,32]{1,3,2,0:T(8,128)(2,1)} %get-tuple-element.208, s32[]{:T(128)} %get-tuple-element.193), kind=kOutput, calls=%fused_computation.4.clone.1 | convolution fusion | flops 281010176 | bytes 17597440 | tf_op jit(solution)/shard_map/while/body/eval_jaxpr/qhe,khe->qhk/dot_general | solution.py:30
  193.8 8.5 %fusion.118 = f32[1024,8]{0,1:T(8,128)S(1)} fusion(f32[8,512,1024]{2,1,0:T(8,128)} %get-tuple-element.180, f32[1024,8]{0,1:T(8,128)S(1)} %select_maximum_fusion.2, pred[512]{0:T(512)(128)(4,1)S(1)} %compare_reduce_fusion.2), kind=kLoop, calls=%fused_computation.9.clone.1 | loop fusion | flops 20963328 | bytes 16843264 | tf_op jit(solution)/shard_map/while/body/eval_jaxpr/reduce_sum | solution.py:38
  209.3 8.8 %bitcast_reduce_fusion.2 = (f32[1024,8]{0,1:T(8,128)S(1)}, f32[8,512,1024]{2,1,0:T(8,128)}) fusion(pred[512]{0:T(512)(128)(4,1)S(1)} %compare_reduce_fusion.2, bf16[1024,8,32]{0,2,1:T(8,128)(2,1)S(1)} %get-tuple-element.209, bf16[16,512,8,32]{1,3,2,0:T(8,128)(2,1)} %get-tuple-element.208, s32[]{:T(128)} %get-tuple-element.193), kind=kOutput, calls=%fused_computation.4.clone.1 | convolution fusion | flops 281010176 | bytes 17597440 | tf_op jit(solution)/shard_map/while/body/eval_jaxpr/qhe,khe->qhk/dot_general | solution.py:30
  218.1 8.5 %fusion.118 = f32[1024,8]{0,1:T(8,128)S(1)} fusion(f32[8,512,1024]{2,1,0:T(8,128)} %get-tuple-element.180, f32[1024,8]{0,1:T(8,128)S(1)} %select_maximum_fusion.2, pred[512]{0:T(512)(128)(4,1)S(1)} %compare_reduce_fusion.2), kind=kLoop, calls=%fused_computation.9.clone.1 | loop fusion | flops 20963328 | bytes 16843264 | tf_op jit(solution)/shard_map/while/body/eval_jaxpr/reduce_sum | solution.py:38
  228.7 4.8 fusion.120
  233.6 8.8 %bitcast_reduce_fusion.2 = (f32[1024,8]{0,1:T(8,128)S(1)}, f32[8,512,1024]{2,1,0:T(8,128)}) fusion(pred[512]{0:T(512)(128)(4,1)S(1)} %compare_reduce_fusion.2, bf16[1024,8,32]{0,2,1:T(8,128)(2,1)S(1)} %get-tuple-element.209, bf16[16,512,8,32]{1,3,2,0:T(8,128)(2,1)} %get-tuple-element.208, s32[]{:T(128)} %get-tuple-element.193), kind=kOutput, calls=%fused_computation.4.clone.1 | convolution fusion | flops 281010176 | bytes 17597440 | tf_op jit(solution)/shard_map/while/body/eval_jaxpr/qhe,khe->qhk/dot_general | solution.py:30
  242.4 8.5 %fusion.118 = f32[1024,8]{0,1:T(8,128)S(1)} fusion(f32[8,512,1024]{2,1,0:T(8,128)} %get-tuple-element.180, f32[1024,8]{0,1:T(8,128)S(1)} %select_maximum_fusion.2, pred[512]{0:T(512)(128)(4,1)S(1)} %compare_reduce_fusion.2), kind=kLoop, calls=%fused_computation.9.clone.1 | loop fusion | flops 20963328 | bytes 16843264 | tf_op jit(solution)/shard_map/while/body/eval_jaxpr/reduce_sum | solution.py:38
  253.0 4.8 fusion.120
  257.8 8.8 %bitcast_reduce_fusion.2 = (f32[1024,8]{0,1:T(8,128)S(1)}, f32[8,512,1024]{2,1,0:T(8,128)}) fusion(pred[512]{0:T(512)(128)(4,1)S(1)} %compare_reduce_fusion.2, bf16[1024,8,32]{0,2,1:T(8,128)(2,1)S(1)} %get-tuple-element.209, bf16[16,512,8,32]{1,3,2,0:T(8,128)(2,1)} %get-tuple-element.208, s32[]{:T(128)} %get-tuple-element.193), kind=kOutput, calls=%fused_computation.4.clone.1 | convolution fusion | flops 281010176 | bytes 17597440 | tf_op jit(solution)/shard_map/while/body/eval_jaxpr/qhe,khe->qhk/dot_general | solution.py:30
  266.6 8.5 %fusion.118 = f32[1024,8]{0,1:T(8,128)S(1)} fusion(f32[8,512,1024]{2,1,0:T(8,128)} %get-tuple-element.180, f32[1024,8]{0,1:T(8,128)S(1)} %select_maximum_fusion.2, pred[512]{0:T(512)(128)(4,1)S(1)} %compare_reduce_fusion.2), kind=kLoop, calls=%fused_computation.9.clone.1 | loop fusion | flops 20963328 | bytes 16843264 | tf_op jit(solution)/shard_map/while/body/eval_jaxpr/reduce_sum | solution.py:38
  282.1 8.8 %bitcast_reduce_fusion.2 = (f32[1024,8]{0,1:T(8,128)S(1)}, f32[8,512,1024]{2,1,0:T(8,128)}) fusion(pred[512]{0:T(512)(128)(4,1)S(1)} %compare_reduce_fusion.2, bf16[1024,8,32]{0,2,1:T(8,128)(2,1)S(1)} %get-tuple-element.209, bf16[16,512,8,32]{1,3,2,0:T(8,128)(2,1)} %get-tuple-element.208, s32[]{:T(128)} %get-tuple-element.193), kind=kOutput, calls=%fused_computation.4.clone.1 | convolution fusion | flops 281010176 | bytes 17597440 | tf_op jit(solution)/shard_map/while/body/eval_jaxpr/qhe,khe->qhk/dot_general | solution.py:30
  290.9 8.5 %fusion.118 = f32[1024,8]{0,1:T(8,128)S(1)} fusion(f32[8,512,1024]{2,1,0:T(8,128)} %get-tuple-element.180, f32[1024,8]{0,1:T(8,128)S(1)} %select_maximum_fusion.2, pred[512]{0:T(512)(128)(4,1)S(1)} %compare_reduce_fusion.2), kind=kLoop, calls=%fused_computation.9.clone.1 | loop fusion | flops 20963328 | bytes 16843264 | tf_op jit(solution)/shard_map/while/body/eval_jaxpr/reduce_sum | solution.py:38
  301.5 4.8 fusion.120
  306.4 8.8 %bitcast_reduce_fusion.2 = (f32[1024,8]{0,1:T(8,128)S(1)}, f32[8,512,1024]{2,1,0:T(8,128)}) fusion(pred[512]{0:T(512)(128)(4,1)S(1)} %compare_reduce_fusion.2, bf16[1024,8,32]{0,2,1:T(8,128)(2,1)S(1)} %get-tuple-element.209, bf16[16,512,8,32]{1,3,2,0:T(8,128)(2,1)} %get-tuple-element.208, s32[]{:T(128)} %get-tuple-element.193), kind=kOutput, calls=%fused_computation.4.clone.1 | convolution fusion | flops 281010176 | bytes 17597440 | tf_op jit(solution)/shard_map/while/body/eval_jaxpr/qhe,khe->qhk/dot_general | solution.py:30
  315.2 8.5 %fusion.118 = f32[1024,8]{0,1:T(8,128)S(1)} fusion(f32[8,512,1024]{2,1,0:T(8,128)} %get-tuple-element.180, f32[1024,8]{0,1:T(8,128)S(1)} %select_maximum_fusion.2, pred[512]{0:T(512)(128)(4,1)S(1)} %compare_reduce_fusion.2), kind=kLoop, calls=%fused_computation.9.clone.1 | loop fusion | flops 20963328 | bytes 16843264 | tf_op jit(solution)/shard_map/while/body/eval_jaxpr/reduce_sum | solution.py:38
  330.7 8.8 %bitcast_reduce_fusion.2 = (f32[1024,8]{0,1:T(8,128)S(1)}, f32[8,512,1024]{2,1,0:T(8,128)}) fusion(pred[512]{0:T(512)(128)(4,1)S(1)} %compare_reduce_fusion.2, bf16[1024,8,32]{0,2,1:T(8,128)(2,1)S(1)} %get-tuple-element.209, bf16[16,512,8,32]{1,3,2,0:T(8,128)(2,1)} %get-tuple-element.208, s32[]{:T(128)} %get-tuple-element.193), kind=kOutput, calls=%fused_computation.4.clone.1 | convolution fusion | flops 281010176 | bytes 17597440 | tf_op jit(solution)/shard_map/while/body/eval_jaxpr/qhe,khe->qhk/dot_general | solution.py:30
  339.5 8.5 %fusion.118 = f32[1024,8]{0,1:T(8,128)S(1)} fusion(f32[8,512,1024]{2,1,0:T(8,128)} %get-tuple-element.180, f32[1024,8]{0,1:T(8,128)S(1)} %select_maximum_fusion.2, pred[512]{0:T(512)(128)(4,1)S(1)} %compare_reduce_fusion.2), kind=kLoop, calls=%fused_computation.9.clone.1 | loop fusion | flops 20963328 | bytes 16843264 | tf_op jit(solution)/shard_map/while/body/eval_jaxpr/reduce_sum | solution.py:38
  355.0 8.8 %bitcast_reduce_fusion.2 = (f32[1024,8]{0,1:T(8,128)S(1)}, f32[8,512,1024]{2,1,0:T(8,128)}) fusion(pred[512]{0:T(512)(128)(4,1)S(1)} %compare_reduce_fusion.2, bf16[1024,8,32]{0,2,1:T(8,128)(2,1)S(1)} %get-tuple-element.209, bf16[16,512,8,32]{1,3,2,0:T(8,128)(2,1)} %get-tuple-element.208, s32[]{:T(128)} %get-tuple-element.193), kind=kOutput, calls=%fused_computation.4.clone.1 | convolution fusion | flops 281010176 | bytes 17597440 | tf_op jit(solution)/shard_map/while/body/eval_jaxpr/qhe,khe->qhk/dot_general | solution.py:30
  363.8 8.5 %fusion.118 = f32[1024,8]{0,1:T(8,128)S(1)} fusion(f32[8,512,1024]{2,1,0:T(8,128)} %get-tuple-element.180, f32[1024,8]{0,1:T(8,128)S(1)} %select_maximum_fusion.2, pred[512]{0:T(512)(128)(4,1)S(1)} %compare_reduce_fusion.2), kind=kLoop, calls=%fused_computation.9.clone.1 | loop fusion | flops 20963328 | bytes 16843264 | tf_op jit(solution)/shard_map/while/body/eval_jaxpr/reduce_sum | solution.py:38
  374.4 4.8 fusion.120
  379.2 8.8 %bitcast_reduce_fusion.2 = (f32[1024,8]{0,1:T(8,128)S(1)}, f32[8,512,1024]{2,1,0:T(8,128)}) fusion(pred[512]{0:T(512)(128)(4,1)S(1)} %compare_reduce_fusion.2, bf16[1024,8,32]{0,2,1:T(8,128)(2,1)S(1)} %get-tuple-element.209, bf16[16,512,8,32]{1,3,2,0:T(8,128)(2,1)} %get-tuple-element.208, s32[]{:T(128)} %get-tuple-element.193), kind=kOutput, calls=%fused_computation.4.clone.1 | convolution fusion | flops 281010176 | bytes 17597440 | tf_op jit(solution)/shard_map/while/body/eval_jaxpr/qhe,khe->qhk/dot_general | solution.py:30
  388.0 8.5 %fusion.118 = f32[1024,8]{0,1:T(8,128)S(1)} fusion(f32[8,512,1024]{2,1,0:T(8,128)} %get-tuple-element.180, f32[1024,8]{0,1:T(8,128)S(1)} %select_maximum_fusion.2, pred[512]{0:T(512)(128)(4,1)S(1)} %compare_reduce_fusion.2), kind=kLoop, calls=%fused_computation.9.clone.1 | loop fusion | flops 20963328 | bytes 16843264 | tf_op jit(solution)/shard_map/while/body/eval_jaxpr/reduce_sum | solution.py:38
  403.5 8.8 %bitcast_reduce_fusion.2 = (f32[1024,8]{0,1:T(8,128)S(1)}, f32[8,512,1024]{2,1,0:T(8,128)}) fusion(pred[512]{0:T(512)(128)(4,1)S(1)} %compare_reduce_fusion.2, bf16[1024,8,32]{0,2,1:T(8,128)(2,1)S(1)} %get-tuple-element.209, bf16[16,512,8,32]{1,3,2,0:T(8,128)(2,1)} %get-tuple-element.208, s32[]{:T(128)} %get-tuple-element.193), kind=kOutput, calls=%fused_computation.4.clone.1 | convolution fusion | flops 281010176 | bytes 17597440 | tf_op jit(solution)/shard_map/while/body/eval_jaxpr/qhe,khe->qhk/dot_general | solution.py:30
  412.3 8.5 %fusion.118 = f32[1024,8]{0,1:T(8,128)S(1)} fusion(f32[8,512,1024]{2,1,0:T(8,128)} %get-tuple-element.180, f32[1024,8]{0,1:T(8,128)S(1)} %select_maximum_fusion.2, pred[512]{0:T(512)(128)(4,1)S(1)} %compare_reduce_fusion.2), kind=kLoop, calls=%fused_computation.9.clone.1 | loop fusion | flops 20963328 | bytes 16843264 | tf_op jit(solution)/shard_map/while/body/eval_jaxpr/reduce_sum | solution.py:38
  427.8 8.8 %bitcast_reduce_fusion.2 = (f32[1024,8]{0,1:T(8,128)S(1)}, f32[8,512,1024]{2,1,0:T(8,128)}) fusion(pred[512]{0:T(512)(128)(4,1)S(1)} %compare_reduce_fusion.2, bf16[1024,8,32]{0,2,1:T(8,128)(2,1)S(1)} %get-tuple-element.209, bf16[16,512,8,32]{1,3,2,0:T(8,128)(2,1)} %get-tuple-element.208, s32[]{:T(128)} %get-tuple-element.193), kind=kOutput, calls=%fused_computation.4.clone.1 | convolution fusion | flops 281010176 | bytes 17597440 | tf_op jit(solution)/shard_map/while/body/eval_jaxpr/qhe,khe->qhk/dot_general | solution.py:30
  436.6 8.5 %fusion.118 = f32[1024,8]{0,1:T(8,128)S(1)} fusion(f32[8,512,1024]{2,1,0:T(8,128)} %get-tuple-element.180, f32[1024,8]{0,1:T(8,128)S(1)} %select_maximum_fusion.2, pred[512]{0:T(512)(128)(4,1)S(1)} %compare_reduce_fusion.2), kind=kLoop, calls=%fused_computation.9.clone.1 | loop fusion | flops 20963328 | bytes 16843264 | tf_op jit(solution)/shard_map/while/body/eval_jaxpr/reduce_sum | solution.py:38
  447.2 4.8 fusion.120
  452.1 8.8 %bitcast_reduce_fusion.2 = (f32[1024,8]{0,1:T(8,128)S(1)}, f32[8,512,1024]{2,1,0:T(8,128)}) fusion(pred[512]{0:T(512)(128)(4,1)S(1)} %compare_reduce_fusion.2, bf16[1024,8,32]{0,2,1:T(8,128)(2,1)S(1)} %get-tuple-element.209, bf16[16,512,8,32]{1,3,2,0:T(8,128)(2,1)} %get-tuple-element.208, s32[]{:T(128)} %get-tuple-element.193), kind=kOutput, calls=%fused_computation.4.clone.1 | convolution fusion | flops 281010176 | bytes 17597440 | tf_op jit(solution)/shard_map/while/body/eval_jaxpr/qhe,khe->qhk/dot_general | solution.py:30
  460.9 8.5 %fusion.118 = f32[1024,8]{0,1:T(8,128)S(1)} fusion(f32[8,512,1024]{2,1,0:T(8,128)} %get-tuple-element.180, f32[1024,8]{0,1:T(8,128)S(1)} %select_maximum_fusion.2, pred[512]{0:T(512)(128)(4,1)S(1)} %compare_reduce_fusion.2), kind=kLoop, calls=%fused_computation.9.clone.1 | loop fusion | flops 20963328 | bytes 16843264 | tf_op jit(solution)/shard_map/while/body/eval_jaxpr/reduce_sum | solution.py:38
  471.5 4.8 fusion.120
  476.4 8.8 %bitcast_reduce_fusion.2 = (f32[1024,8]{0,1:T(8,128)S(1)}, f32[8,512,1024]{2,1,0:T(8,128)}) fusion(pred[512]{0:T(512)(128)(4,1)S(1)} %compare_reduce_fusion.2, bf16[1024,8,32]{0,2,1:T(8,128)(2,1)S(1)} %get-tuple-element.209, bf16[16,512,8,32]{1,3,2,0:T(8,128)(2,1)} %get-tuple-element.208, s32[]{:T(128)} %get-tuple-element.193), kind=kOutput, calls=%fused_computation.4.clone.1 | convolution fusion | flops 281010176 | bytes 17597440 | tf_op jit(solution)/shard_map/while/body/eval_jaxpr/qhe,khe->qhk/dot_general | solution.py:30
  485.2 8.5 %fusion.118 = f32[1024,8]{0,1:T(8,128)S(1)} fusion(f32[8,512,1024]{2,1,0:T(8,128)} %get-tuple-element.180, f32[1024,8]{0,1:T(8,128)S(1)} %select_maximum_fusion.2, pred[512]{0:T(512)(128)(4,1)S(1)} %compare_reduce_fusion.2), kind=kLoop, calls=%fused_computation.9.clone.1 | loop fusion | flops 20963328 | bytes 16843264 | tf_op jit(solution)/shard_map/while/body/eval_jaxpr/reduce_sum | solution.py:38
  501.9 10.6 %fusion.46 = bf16[128,8,256]{2,1,0:T(8,128)(2,1)} fusion(f32[1024,256]{1,0:T(8,128)S(1)} %get-tuple-element.125, bf16[1024,256]{1,0:T(8,128)(2,1)S(1)} %copy-done, bf16[256,1024]{1,0:T(8,128)(2,1)S(1)} %copy-done.3, f32[256]{0:T(256)S(1)} %copy-done.4, f32[1024]{0:T(1024)S(1)} %add_rsqrt_fusion.1, f32[1024]{0:T(1024)S(1)} %broadcast_multiply_fusion.1), kind=kOutput, calls=%fused_computation.60 | convolution fusion | flops 1143472128 | bytes 2630656 | tf_op jit(solution)/shard_map/dot_general | solution.py:114
  512.5 7.8 %all-to-all-start.2 = ((bf16[128,8,256]{2,1,0:T(8,128)(2,1)}), bf16[128,8,256]{2,1,0:T(8,128)(2,1)S(1)}, u32[]{:S(2)}, u32[]{:S(2)}) async-start(bf16[128,8,256]{2,1,0:T(8,128)(2,1)} %fusion.46), calls=%async_computation.2 | async-start | bytes 1048576 | tf_op jit(solution)/shard_map/all_to_all | solution.py:117
  520.4 13.7 %all-to-all-done.2 = bf16[128,8,256]{2,1,0:T(8,128)(2,1)S(1)} async-done(((bf16[128,8,256]{2,1,0:T(8,128)(2,1)}), bf16[128,8,256]{2,1,0:T(8,128)(2,1)S(1)}, u32[]{:S(2)}, u32[]{:S(2)}) %all-to-all-start.2) | async-done | bytes 524320 | tf_op jit(solution)/shard_map/all_to_all | solution.py:117
  (150 shorter events, 110.9 us)
Async XLA Ops:
  6.5 495.3 %copy-start = (bf16[1024,256]{1,0:T(8,128)(2,1)S(1)}, bf16[1024,256]{1,0:T(8,128)(2,1)}, u32[]{:S(2)}) copy-start(bf16[1024,256]{1,0:T(8,128)(2,1)} %param.17) | copy-start | bytes 1572868
  6.5 65.6 %all-gather.3.cloned.1.call-start = ((), (), s32[]{:S(2)}) async-start(), calls=%async_computation.3 | async-start | bytes 4718592 | tf_op jit(solution)/shard_map/all_gather | solution.py:101
  40.2 63.3 %all-gather.5.cloned.1.call-start = ((), (), s32[]{:S(2)}) async-start(), calls=%async_computation.4 | async-start | bytes 4718592 | tf_op jit(solution)/shard_map/all_gather | solution.py:102
  45.5 14.2 %all-to-all-start.1 = ((bf16[128,1,8]{2,1,0:T(2,128)(2,1)}), bf16[128,1,8]{2,1,0:T(2,128)(2,1)S(1)}, u32[]{:S(2)}, u32[]{:S(2)}) async-start(bf16[128,1,8]{2,1,0:T(2,128)(2,1)} %all_to_all.16), calls=%async_computation.1 | async-start | bytes 131072 | tf_op jit(solution)/shard_map/all_to_all | solution.py:82
  111.9 389.1 %copy-start.2 = (bf16[256,256]{1,0:T(8,128)(2,1)S(1)}, bf16[256,256]{1,0:T(8,128)(2,1)}, u32[]{:S(2)}) copy-start(bf16[256,256]{1,0:T(8,128)(2,1)} %param.14) | copy-start | bytes 393220
  120.9 10.6 %copy-start.1 = (f32[8,512,1024]{2,1,0:T(8,128)S(1)}, f32[8,512,1024]{2,1,0:T(8,128)}, u32[]{:S(2)}) copy-start(f32[8,512,1024]{2,1,0:T(8,128)} %get-tuple-element.180) | copy-start | bytes 50331652 | tf_op jit(solution)/shard_map/while
  145.2 10.6 %copy-start.1 = (f32[8,512,1024]{2,1,0:T(8,128)S(1)}, f32[8,512,1024]{2,1,0:T(8,128)}, u32[]{:S(2)}) copy-start(f32[8,512,1024]{2,1,0:T(8,128)} %get-tuple-element.180) | copy-start | bytes 50331652 | tf_op jit(solution)/shard_map/while
  169.5 10.6 %copy-start.1 = (f32[8,512,1024]{2,1,0:T(8,128)S(1)}, f32[8,512,1024]{2,1,0:T(8,128)}, u32[]{:S(2)}) copy-start(f32[8,512,1024]{2,1,0:T(8,128)} %get-tuple-element.180) | copy-start | bytes 50331652 | tf_op jit(solution)/shard_map/while
  193.8 10.6 %copy-start.1 = (f32[8,512,1024]{2,1,0:T(8,128)S(1)}, f32[8,512,1024]{2,1,0:T(8,128)}, u32[]{:S(2)}) copy-start(f32[8,512,1024]{2,1,0:T(8,128)} %get-tuple-element.180) | copy-start | bytes 50331652 | tf_op jit(solution)/shard_map/while
  218.1 10.6 %copy-start.1 = (f32[8,512,1024]{2,1,0:T(8,128)S(1)}, f32[8,512,1024]{2,1,0:T(8,128)}, u32[]{:S(2)}) copy-start(f32[8,512,1024]{2,1,0:T(8,128)} %get-tuple-element.180) | copy-start | bytes 50331652 | tf_op jit(solution)/shard_map/while
  242.4 10.6 %copy-start.1 = (f32[8,512,1024]{2,1,0:T(8,128)S(1)}, f32[8,512,1024]{2,1,0:T(8,128)}, u32[]{:S(2)}) copy-start(f32[8,512,1024]{2,1,0:T(8,128)} %get-tuple-element.180) | copy-start | bytes 50331652 | tf_op jit(solution)/shard_map/while
  266.6 10.6 %copy-start.1 = (f32[8,512,1024]{2,1,0:T(8,128)S(1)}, f32[8,512,1024]{2,1,0:T(8,128)}, u32[]{:S(2)}) copy-start(f32[8,512,1024]{2,1,0:T(8,128)} %get-tuple-element.180) | copy-start | bytes 50331652 | tf_op jit(solution)/shard_map/while
  290.9 10.6 %copy-start.1 = (f32[8,512,1024]{2,1,0:T(8,128)S(1)}, f32[8,512,1024]{2,1,0:T(8,128)}, u32[]{:S(2)}) copy-start(f32[8,512,1024]{2,1,0:T(8,128)} %get-tuple-element.180) | copy-start | bytes 50331652 | tf_op jit(solution)/shard_map/while
  315.2 10.6 %copy-start.1 = (f32[8,512,1024]{2,1,0:T(8,128)S(1)}, f32[8,512,1024]{2,1,0:T(8,128)}, u32[]{:S(2)}) copy-start(f32[8,512,1024]{2,1,0:T(8,128)} %get-tuple-element.180) | copy-start | bytes 50331652 | tf_op jit(solution)/shard_map/while
  339.5 10.6 %copy-start.1 = (f32[8,512,1024]{2,1,0:T(8,128)S(1)}, f32[8,512,1024]{2,1,0:T(8,128)}, u32[]{:S(2)}) copy-start(f32[8,512,1024]{2,1,0:T(8,128)} %get-tuple-element.180) | copy-start | bytes 50331652 | tf_op jit(solution)/shard_map/while
  363.8 10.6 %copy-start.1 = (f32[8,512,1024]{2,1,0:T(8,128)S(1)}, f32[8,512,1024]{2,1,0:T(8,128)}, u32[]{:S(2)}) copy-start(f32[8,512,1024]{2,1,0:T(8,128)} %get-tuple-element.180) | copy-start | bytes 50331652 | tf_op jit(solution)/shard_map/while
  388.0 10.6 %copy-start.1 = (f32[8,512,1024]{2,1,0:T(8,128)S(1)}, f32[8,512,1024]{2,1,0:T(8,128)}, u32[]{:S(2)}) copy-start(f32[8,512,1024]{2,1,0:T(8,128)} %get-tuple-element.180) | copy-start | bytes 50331652 | tf_op jit(solution)/shard_map/while
  412.3 10.6 %copy-start.1 = (f32[8,512,1024]{2,1,0:T(8,128)S(1)}, f32[8,512,1024]{2,1,0:T(8,128)}, u32[]{:S(2)}) copy-start(f32[8,512,1024]{2,1,0:T(8,128)} %get-tuple-element.180) | copy-start | bytes 50331652 | tf_op jit(solution)/shard_map/while
  436.6 10.6 %copy-start.1 = (f32[8,512,1024]{2,1,0:T(8,128)S(1)}, f32[8,512,1024]{2,1,0:T(8,128)}, u32[]{:S(2)}) copy-start(f32[8,512,1024]{2,1,0:T(8,128)} %get-tuple-element.180) | copy-start | bytes 50331652 | tf_op jit(solution)/shard_map/while
  460.9 10.6 %copy-start.1 = (f32[8,512,1024]{2,1,0:T(8,128)S(1)}, f32[8,512,1024]{2,1,0:T(8,128)}, u32[]{:S(2)}) copy-start(f32[8,512,1024]{2,1,0:T(8,128)} %get-tuple-element.180) | copy-start | bytes 50331652 | tf_op jit(solution)/shard_map/while
  485.2 10.6 %copy-start.1 = (f32[8,512,1024]{2,1,0:T(8,128)S(1)}, f32[8,512,1024]{2,1,0:T(8,128)}, u32[]{:S(2)}) copy-start(f32[8,512,1024]{2,1,0:T(8,128)} %get-tuple-element.180) | copy-start | bytes 50331652 | tf_op jit(solution)/shard_map/while
  500.9 1.0 copy-start.3
  500.9 1.0 copy-start.4
  512.5 21.6 %all-to-all-start.2 = ((bf16[128,8,256]{2,1,0:T(8,128)(2,1)}), bf16[128,8,256]{2,1,0:T(8,128)(2,1)S(1)}, u32[]{:S(2)}, u32[]{:S(2)}) async-start(bf16[128,8,256]{2,1,0:T(8,128)(2,1)} %fusion.46), calls=%async_computation.2 | async-start | bytes 1048576 | tf_op jit(solution)/shard_map/all_to_all | solution.py:117
Sparse Core Ops, SparseCore 0:
  40.3 29.4 all-gather.2
  71.5 31.9 all-gather.4
where the time goes:
time: 552 us; the launch traced here: 544 us
  matrix products  232 us (42%)
  other arithmetic  140 us (25%)
  local copies, waits for them, and re-layouts  60.8 us (11%)
  waiting for transfers between devices  47.2 us (9%)
  blocking collectives  37.1 us (7%)
  between operations  14 us (3%)
  starting transfers between devices  12.4 us (2%)
    dot_general x16, matrix products, step(): jnp.einsum('qhe,khe->qhk', queries, key_block, preferred_element_type=jnp...  140 us
    reduce_sum x16, other arithmetic, step(): new_total = running_total * factor + jnp.sum(weights, axis=2)  137 us
    dot_general x16, matrix products, step(): jnp.einsum('qhk,khe->qhe', weights.astype(jnp.bfloat16), value_block, pre...  77.1 us
    while x48, local copies, waits for them, and re-layouts  32.5 us
    all_to_all x1, blocking collectives, local(): lax.all_to_all(outgoing.reshape(dev_count, capacity, model_width), ('regi...  25 us
    all_gather x1, waiting for transfers between devices, local(): lax.all_gather(projected[:, 2 * D:], 'loop', axis=0, tiled=True)  23 us
    unnamed x12, local copies, waits for them, and re-layouts  16.8 us
    all_to_all x1, waiting for transfers between devices, local(): lax.all_to_all(result.reshape(dev_count, capacity, model_width), ('region...  13.7 us
  transfers between devices with their start and end apart: 4, of which 3 were waited for; matrix products, arithmetic and copies ran while one was open for 2% of the time, Pallas kernels for 0%

commit v1 on v0

v1 whole, which is shorter than its diff:
```python
import functools
import math

import jax
import jax.numpy as jnp
from jax import lax
from jax.experimental import pallas as pl
from jax.experimental.pallas import tpu as pltpu
from jax.sharding import PartitionSpec as P

HEADS = 8
CAP = 8
MARK = 16.0
MESH = pl.DeviceIdType.MESH
EXTRA = 16
F32 = jnp.float32
BF16 = jnp.bfloat16


def iota(shape, dim):
    return lax.broadcasted_iota(jnp.int32, shape, dim)


def one_hot(condition):
    return jnp.where(condition, 1.0, 0.0).astype(BF16)


def route_kernel(
    regions, loops, tokens_ref, dest_ref, pool_ref, place_ref, rank_ref,
    outbox, inbox, packed, send_a, recv_a, send_g, recv_g, local_sem,
):
    rows, width = tokens_ref.shape
    chunk = CAP * loops
    slots = regions * chunk
    chips = loops // 2
    region, loop = lax.axis_index("region"), lax.axis_index("loop")
    chip, core = loop // 2, lax.rem(loop, 2)
    sibling = chip * 2 + (1 - core)
    right = lax.rem(chip + 1, chips) * 2 + core
    left = lax.rem(chip + chips - 1, chips) * 2 + core
    far = lax.rem(chip + 2, chips) * 2 + core

    barrier = pltpu.get_barrier_semaphore()
    for k in range(1, regions):
        pl.semaphore_signal(
            barrier, inc=1, device_id=(lax.rem(region + k, regions), loop), device_id_type=MESH
        )
    for peer in (sibling, left, right):
        pl.semaphore_signal(barrier, inc=1, device_id=(region, peer), device_id_type=MESH)

    owner_region = dest_ref[...] // loops
    hot = one_hot(owner_region == iota((regions, rows), 0))
    upper = one_hot(iota((rows, rows), 0) <= iota((rows, rows), 1))
    before = jnp.dot(hot, upper, preferred_element_type=F32)
    rank = jnp.sum(before * hot.astype(F32), axis=0, keepdims=True).astype(jnp.int32) - 1
    place = owner_region * chunk + rank
    place_ref[...] = jnp.broadcast_to(place, place_ref.shape)
    spread = one_hot(iota((slots, rows), 0) == place)
    sorted_rows = jnp.dot(spread, tokens_ref[...], preferred_element_type=F32)
    held = jnp.dot(spread, jnp.ones((rows, width), BF16), preferred_element_type=F32)
    outbox[...] = (sorted_rows + (1.0 - held) * MARK).astype(BF16)

    pl.semaphore_wait(barrier, regions - 1 + 3)

    def exchange(k):
        peer = lax.rem(region + k, regions)
        return pltpu.make_async_remote_copy(
            src_ref=outbox.at[pl.ds(pl.multiple_of(peer * chunk, chunk), chunk)],
            dst_ref=inbox.at[pl.ds(pl.multiple_of(region * chunk, chunk), chunk)],
            send_sem=send_a.at[k],
            recv_sem=recv_a.at[k],
            device_id=(peer, loop),
            device_id_type=MESH,
        )

    exchanges = [exchange(k) for k in range(1, regions)]
    for copy in exchanges:
        copy.start()
    own = pl.ds(pl.multiple_of(region * chunk, chunk), chunk)
    inbox[own, :] = outbox[own, :]
    earlier = one_hot(iota((slots, slots), 0) < iota((slots, slots), 1))
    for copy in exchanges:
        copy.wait_recv()

    alive = jnp.where(inbox[:, :128].astype(F32) < 8.0, 1.0, 0.0)
    alive_row = alive.T[:16, :]
    ahead = jnp.dot(alive_row.astype(BF16), earlier, preferred_element_type=F32)
    slot = jnp.where(alive_row > 0.0, ahead, -1.0).astype(jnp.int32)
    rank_ref[...] = slot[:8, :]
    squeeze = one_hot(iota((slots, slots), 0) == slot[0:1, :])
    packed[pl.ds(0, slots), :] = jnp.dot(
        squeeze, inbox[...], preferred_element_type=F32
    ).astype(BF16)
    count = jnp.sum(alive_row, axis=1, keepdims=True)
    high = jnp.floor(count * (1.0 / 128.0))
    packed[pl.ds(slots, EXTRA), :] = jnp.where(
        iota((EXTRA, width), 1) < 128, high, count - 128.0 * high
    ).astype(BF16)

    half0, half1 = pl.ds(0, slots // 2), pl.ds(slots // 2, slots // 2 + EXTRA)
    whole = pl.ds(0, slots + EXTRA)

    def move(n, src, slot_index, part, peer):
        copy = pltpu.make_async_remote_copy(
            src_ref=src.at[part],
            dst_ref=pool_ref.at[slot_index, part],
            send_sem=send_g.at[n],
            recv_sem=recv_g.at[n],
            device_id=(region, peer),
            device_id_type=MESH,
        )
        copy.start()
        return copy

    started = [
        move(0, packed, loop, half0, right),
        move(1, packed, loop, half1, left),
        move(2, packed, loop, half1, right),
        move(3, packed, loop, half0, left),
        move(4, packed, loop, whole, sibling),
    ]
    keep = pltpu.make_async_copy(packed, pool_ref.at[loop], local_sem)
    keep.start()
    started[0].wait_recv()
    started.append(move(5, pool_ref.at[left], left, half0, right))
    started.append(move(6, pool_ref.at[left], left, half0, sibling))
    started[1].wait_recv()
    started.append(move(7, pool_ref.at[right], right, half1, left))
    started.append(move(8, pool_ref.at[right], right, half1, sibling))
    started[2].wait_recv()
    started.append(move(9, pool_ref.at[left], left, half1, sibling))
    started[3].wait_recv()
    started.append(move(10, pool_ref.at[right], right, half0, sibling))
    started[5].wait_recv()
    started.append(move(11, pool_ref.at[far], far, half0, sibling))
    started[7].wait_recv()
    started.append(move(12, pool_ref.at[far], far, half1, sibling))
    for n in (4, 6, 8, 9, 10, 11, 12):
        started[n].wait_recv()
    for copy in exchanges + started:
        copy.wait_send()
    keep.wait()


def normalize(values, gain):
    mean = jnp.mean(values, axis=-1, keepdims=True)
    centered = values - mean
    variance = jnp.mean(centered * centered, axis=-1, keepdims=True)
    return centered * lax.rsqrt(variance + 1e-05) * gain


def attend_kernel(
    slots, tq, big, small,
    pool_ref, gain1_ref, wqkv_ref, wout_ref, gain2_ref, whid_ref, wback_ref, out_ref,
    keys, vals_a, vals_b, stacked, accum, top, key_norm,
):
    loops = pool_ref.shape[0]
    width = gain1_ref.shape[1]
    head = width // HEADS
    kt = min(256, slots)
    scale = math.log2(math.e) / math.sqrt(head)
    me = lax.axis_index("loop")
    gain1, gain2 = gain1_ref[...], gain2_ref[...]

    def even_lane(shape):
        return lax.rem(iota(shape, 1) // head, 2) == 0

    def live_rows(j):
        note = pool_ref[j, pl.ds(slots, EXTRA), :].astype(F32)
        high, low = jnp.max(note[:, :128]), jnp.max(note[:, 128:])
        return (high * 128.0 + low).astype(jnp.int32)

    to_head = one_hot(iota((width, 128), 0) // head == iota((width, 128), 1))
    key_norm[...] = jnp.zeros_like(key_norm)

    def project(j, base):
        count = live_rows(j)

        def tile(t, carry):
            start = pl.multiple_of(t * kt, kt)
            x = pool_ref[j, pl.ds(start, kt), :].astype(F32)
            normed = normalize(x, gain1).astype(BF16)
            kv = jnp.dot(normed, wqkv_ref[:, width:], preferred_element_type=F32)
            k = kv[:, :width].astype(BF16)
            v = kv[:, width:]
            valid = iota((kt, width), 0) + start < count
            even = even_lane((kt, width))
            at = pl.ds(pl.multiple_of(base + start, 16), kt)
            keys[at, :] = k
            vals_a[at, :] = jnp.where(valid, jnp.where(even, v, 1.0), 0.0).astype(BF16)
            vals_b[at, :] = jnp.where(valid, jnp.where(even, 1.0, v), 0.0).astype(BF16)
            square = k.astype(F32)
            norms = jnp.dot((square * square).astype(BF16), to_head, preferred_element_type=F32)
            key_norm[...] = jnp.maximum(
                key_norm[...], jnp.max(norms.reshape(kt // 8, 8, 128), axis=0)
            )
            return carry

        lax.fori_loop(0, pl.cdiv(count, kt), tile, 0)
        return base + pl.cdiv(count, 16) * 16

    total_rows = lax.fori_loop(0, loops, project, jnp.int32(0))
    tail = pl.ds(pl.multiple_of(total_rows, 16), small)
    for ref in (keys, vals_a, vals_b):
        ref[tail, :] = jnp.zeros((small, width), BF16)
    key_top = jnp.max(key_norm[...], axis=0, keepdims=True)
    small_count = pl.cdiv(total_rows, small)
    big_count = small_count // (big // small)
    small_first = big_count * (big // small)

    out_ref[...] = jnp.zeros_like(out_ref)
    mine = live_rows(me)
    flag_lane = one_hot(iota((8, width), 1) == head)
    order = tuple(range(0, HEADS, 2)) + tuple(range(1, HEADS, 2))
    group = HEADS // 2 * tq

    def queries(i, carry):
        start = pl.multiple_of(i * tq, tq)
        x = pool_ref[me, pl.ds(start, tq), :].astype(F32)
        normed = normalize(x, gain1).astype(BF16)
        q = jnp.dot(normed, wqkv_ref[:, :width], preferred_element_type=F32).astype(BF16)
        lane_head = iota((tq, width), 1) // head
        for n, h in enumerate(order):
            stacked[n * tq : (n + 1) * tq, :] = jnp.where(lane_head == h, q, jnp.zeros_like(q))
        square = q.astype(F32)
        norms = jnp.dot((square * square).astype(BF16), to_head, preferred_element_type=F32)
        bound = jnp.max(jnp.max(norms, axis=0, keepdims=True) * key_top)
        accum[...] = jnp.zeros_like(accum)

        def scores(at, rows):
            return scale * lax.dot_general(
                stacked[rows, :], keys[at, :], (((1,), (1,)), ((), ())), preferred_element_type=F32
            )

        def plain(size, first):
            def step(j, carry):
                at = pl.ds(pl.multiple_of((first + j) * size, size), size)
                for rows, vals in (
                    (slice(0, group), vals_a),
                    (slice(group, 2 * group), vals_b),
                ):
                    weights = jnp.exp2(scores(at, rows)).astype(BF16)
                    accum[rows, :] += jnp.dot(weights, vals[at, :], preferred_element_type=F32)
                return carry

            return step

        def shifted(j, carry):
            at = pl.ds(pl.multiple_of(j * small, small), small)
            flags = lax.dot_general(
                flag_lane, vals_a[at, :], (((1,), (1,)), ((), ())), preferred_element_type=F32
            )
            live = flags[0:1, :] > 0.5
            for rows, vals in ((slice(0, group), vals_a), (slice(group, 2 * group), vals_b)):
                values = jnp.where(live, scores(at, rows), -1e30)
                old = top[rows, :]
                new = jnp.maximum(old, jnp.max(values, axis=1, keepdims=True))
                top[rows, :] = new
                factor = jnp.exp2(old - new)
                weights = jnp.exp2(values - new[:, :1]).astype(BF16)
                accum[rows, :] = accum[rows, :] * factor[:, :1] + jnp.dot(
                    weights, vals[at, :], preferred_element_type=F32
                )
            return carry

        unshifted = bound * (1.05 * scale * scale) < 4096.0

        @pl.when(unshifted)
        def _():
            lax.fori_loop(0, big_count, plain(big, 0), 0)
            lax.fori_loop(0, small_count - small_first, plain(small, small_first), 0)

        @pl.when(jnp.logical_not(unshifted))
        def _():
            top[...] = jnp.full(top.shape, -1e30, F32)
            lax.fori_loop(0, small_count, shifted, 0)

        part_a = jnp.zeros((tq, width), F32)
        part_b = jnp.zeros((tq, width), F32)
        pair = iota((tq, width), 1) // (2 * head)
        for n in range(HEADS // 2):
            part_a = jnp.where(pair == n, accum[n * tq : (n + 1) * tq, :], part_a)
            part_b = jnp.where(pair == n, accum[group + n * tq : group + (n + 1) * tq, :], part_b)
        even = even_lane((tq, width))
        numerator = jnp.where(even, part_a, part_b)
        sums = jnp.where(even, part_b, part_a)
        total = jnp.where(
            even, pltpu.roll(sums, width - head, 1), pltpu.roll(sums, head, 1)
        )
        attended = (numerator / total).astype(BF16)
        mixed = x + jnp.dot(attended, wout_ref[...], preferred_element_type=F32)
        normed2 = normalize(mixed, gain2).astype(BF16)
        inner = jnp.dot(normed2, whid_ref[...], preferred_element_type=F32)
        hidden = (0.5 * inner * (1.0 + lax.erf(inner * math.sqrt(0.5)))).astype(BF16)
        result = mixed + jnp.dot(hidden, wback_ref[...], preferred_element_type=F32)
        out_ref[pl.ds(start, tq), :] = result.astype(BF16)
        return carry

    lax.fori_loop(0, pl.cdiv(mine, tq), queries, 0)


def give_back_kernel(
    regions, loops, result_ref, rank_ref, place_ref, out_ref, outbox, inbox, send, recv
):
    rows = out_ref.shape[0]
    chunk = CAP * loops
    slots = regions * chunk
    region, loop = lax.axis_index("region"), lax.axis_index("loop")
    barrier = pltpu.get_barrier_semaphore()
    for k in range(1, regions):
        pl.semaphore_signal(
            barrier, inc=1, device_id=(lax.rem(region + k, regions), loop), device_id_type=MESH
        )

    def column(row_ref):
        size = row_ref.shape[1]
        row = jnp.broadcast_to(row_ref[0:1, :].astype(F32), (128, size))
        return row.T[:, 0:1].astype(jnp.int32)

    unpack = one_hot(column(rank_ref) == iota((slots, slots), 1))
    outbox[...] = jnp.dot(unpack, result_ref[...], preferred_element_type=F32).astype(BF16)
    pl.semaphore_wait(barrier, regions - 1)

    def exchange(k):
        peer = lax.rem(region + k, regions)
        return pltpu.make_async_remote_copy(
            src_ref=outbox.at[pl.ds(pl.multiple_of(peer * chunk, chunk), chunk)],
            dst_ref=inbox.at[pl.ds(pl.multiple_of(region * chunk, chunk), chunk)],
            send_sem=send.at[k],
            recv_sem=recv.at[k],
            device_id=(peer, loop),
            device_id_type=MESH,
        )

    exchanges = [exchange(k) for k in range(1, regions)]
    for copy in exchanges:
        copy.start()
    own = pl.ds(pl.multiple_of(region * chunk, chunk), chunk)
    inbox[own, :] = outbox[own, :]
    take = one_hot(column(place_ref) == iota((rows, slots), 1))
    for copy in exchanges:
        copy.wait_recv()
    out_ref[...] = jnp.dot(take, inbox[...], preferred_element_type=F32).astype(BF16)
    for copy in exchanges:
        copy.wait_send()


def local(tq, big, small, tokens, dest, norm1_gain, w_qkv, w_out, norm2_gain, w_hidden, w_back):
    rows, width = tokens.shape
    regions, loops = lax.axis_size("region"), lax.axis_size("loop")
    chunk = CAP * loops
    slots = regions * chunk
    vmem = pl.BlockSpec(memory_space=pltpu.VMEM)
    params = functools.partial(pltpu.CompilerParams, vmem_limit_bytes=48 * 1024 * 1024)
    pool, place, rank = pl.pallas_call(
        functools.partial(route_kernel, regions, loops),
        out_shape=(
            jax.ShapeDtypeStruct((loops, slots + EXTRA, width), BF16),
            jax.ShapeDtypeStruct((8, rows), jnp.int32),
            jax.ShapeDtypeStruct((8, slots), jnp.int32),
        ),
        in_specs=[vmem] * 2,
        out_specs=(pl.BlockSpec(memory_space=pl.ANY), vmem, vmem),
        scratch_shapes=[
            pltpu.VMEM((slots, width), BF16),
            pltpu.VMEM((slots, width), BF16),
            pltpu.VMEM((slots + EXTRA, width), BF16),
            pltpu.SemaphoreType.DMA((regions,)),
            pltpu.SemaphoreType.DMA((regions,)),
            pltpu.SemaphoreType.DMA((13,)),
            pltpu.SemaphoreType.DMA((13,)),
            pltpu.SemaphoreType.DMA,
        ],
        compiler_params=params(collective_id=0, has_side_effects=True),
        name="route",
    )(tokens, dest.reshape(1, rows))
    key_rows = loops * slots + small + min(256, slots)
    result = pl.pallas_call(
        functools.partial(attend_kernel, slots, tq, big, small),
        out_shape=jax.ShapeDtypeStruct((slots, width), BF16),
        in_specs=[vmem] * 7,
        out_specs=vmem,
        scratch_shapes=[
            pltpu.VMEM((key_rows, width), BF16),
            pltpu.VMEM((key_rows, width), BF16),
            pltpu.VMEM((key_rows, width), BF16),
            pltpu.VMEM((HEADS * tq, width), BF16),
            pltpu.VMEM((HEADS * tq, width), F32),
            pltpu.VMEM((HEADS * tq, 128), F32),
            pltpu.VMEM((8, 128), F32),
        ],
        compiler_params=params(),
        name="attend",
    )(
        pool, norm1_gain.reshape(1, width), w_qkv, w_out, norm2_gain.reshape(1, width),
        w_hidden, w_back,
    )
    return pl.pallas_call(
        functools.partial(give_back_kernel, regions, loops),
        out_shape=jax.ShapeDtypeStruct((rows, width), BF16),
        in_specs=[vmem] * 3,
        out_specs=vmem,
        scratch_shapes=[
            pltpu.VMEM((slots, width), BF16),
            pltpu.VMEM((slots, width), BF16),
            pltpu.SemaphoreType.DMA((regions,)),
            pltpu.SemaphoreType.DMA((regions,)),
        ],
        compiler_params=params(collective_id=1, has_side_effects=True),
        name="give_back",
    )(result, rank, place)


def build(mesh, tq, big, small):
    spread = P(("region", "loop"), None)
    return jax.shard_map(
        functools.partial(local, tq, big, small),
        mesh=mesh,
        in_specs=(spread, spread) + (P(),) * 6,
        out_specs=spread,
        check_vma=False,
    )


def solution(mesh):
    return build(mesh, 256, 2048, 512)
```

time: 552 us -> 205 us (0.37); the launches traced: 544 us -> 205 us
  matrix products: 232 us -> 0 us
  Pallas kernels: 0 us -> 195 us
  other arithmetic: 140 us -> 0 us
  local copies, waits for them, and re-layouts: 60.8 us -> 9.63 us
  waiting for transfers between devices: 47.2 us -> 0 us
  blocking collectives: 37.1 us -> 0 us
  between operations: 14 us -> 0.04 us
  starting transfers between devices: 12.4 us -> 0 us
    dot_general x36 -> x0, matrix products: 232 us -> none  [the longest x16 140 us: step(): jnp.einsum('qhe,khe->qhk', queries, key_block, preferred_element_type=jnp...]
    pallas_call x0 -> x3, Pallas kernels: none -> 195 us  [the longest x1 115 us: local(): pl.pallas_call(functools.partial(attend_kernel, slots, tq, big, small), o...]
    reduce_sum x19 -> x0, other arithmetic: 138 us -> none  [the longest x16 137 us: step(): new_total = running_total * factor + jnp.sum(weights, axis=2)]
    while x48 -> x0, local copies, waits for them, and re-layouts: 32.5 us -> none
    all_to_all x1 -> x0, blocking collectives: 25 us -> none  [local(): lax.all_to_all(outgoing.reshape(dev_count, capacity, model_width), ('regi...]
    all_to_all x2 -> x0, waiting for transfers between devices: 23.4 us -> none  [the longest x1 13.7 us: local(): lax.all_to_all(result.reshape(dev_count, capacity, model_width), ('region...]
    all_gather x2 -> x0, waiting for transfers between devices: 23 us -> none  [the longest x1 23 us: local(): lax.all_gather(projected[:, 2 * D:], 'loop', axis=0, tiled=True)]
    all_to_all x2 -> x0, starting transfers between devices: 12.3 us -> none  [the longest x1 7.84 us: local(): lax.all_to_all(result.reshape(dev_count, capacity, model_width), ('region...]
  transfers between devices with their start and end apart: 4 -> 0, of which waited for: 3 -> 0; matrix products, arithmetic and copies ran while one was open for 2% -> 0% of each run, Pallas kernels for 0% -> 0%
where the time goes in v1:
time: 205 us
  Pallas kernels  195 us (95%)
  local copies, waits for them, and re-layouts  9.63 us (5%)
    pallas_call x1, Pallas kernels, local(): pl.pallas_call(functools.partial(attend_kernel, slots, tq, big, small), o...  115 us
    pallas_call x1, Pallas kernels, local(): pl.pallas_call(functools.partial(give_back_kernel, regions, loops), out_s...  43.4 us
    pallas_call x1, Pallas kernels, local(): pl.pallas_call(functools.partial(route_kernel, regions, loops), out_shape...  37.5 us
    unnamed x19, local copies, waits for them, and re-layouts  9.63 us

profile of v1, /device:TPU:1, one launch (start us, length us, event | category | flops | bytes accessed | tf_op | source)
XLA Modules:
  0.0 205.1 jit_solution(2620450963136080483)
XLA Ops:
  0.0 0.0 copy-start.4
  0.0 0.9 copy-done.4
  1.0 0.0 copy-start.6
  1.0 0.7 copy-done.6
  1.6 37.5 %route.1 = (bf16[8,1040,256]{2,1,0:T(8,128)(2,1)S(1)}, s32[8,512]{1,0:T(8,128)S(1)}, s32[8,1024]{1,0:T(8,128)S(1)}) custom-call(bf16[512,256]{1,0:T(8,128)(2,1)S(1)} %copy-done.4, s32[1,512]{1,0:T(1,128)S(1)} %bitcast.3), custom_call_target="tpu_custom_call" | custom-call | tf_op jit(solution)/shard_map/route/pallas_call | solution.py:355
  39.1 0.0 copy-start
  39.1 2.0 copy-done
  41.1 0.0 copy-start.1
  41.1 1.0 copy-done.1
  42.1 0.0 copy-start.2
  42.1 1.0 copy-done.2
  43.2 0.0 copy-start.3
  43.2 1.0 copy-done.3
  44.2 0.0 copy-start.5
  44.2 0.9 copy-done.5
  45.1 0.0 copy-start.7
  45.1 0.7 copy-done.7
  45.8 0.0 copy-start.8
  45.8 0.7 copy-done.8
  46.4 114.5 %attend.1.result_ref = bf16[1024,256]{1,0:T(8,128)(2,1)S(1)} custom-call(bf16[8,1040,256]{2,1,0:T(8,128)(2,1)} %copy-done, f32[1,256]{1,0:T(1,128)S(1)} %bitcast.4, bf16[256,768]{1,0:T(8,128)(2,1)S(1)} %copy-done.3, bf16[256,256]{1,0:T(8,128)(2,1)S(1)} %copy-done.5, f32[1,256]{1,0:T(1,128)S(1)} %bitcast.5, bf16[256,1024]{1,0:T(8,128)(2,1)S(1)} %copy-done.1, ...), custom_call_target="tpu_custom_call" | custom-call | tf_op jit(solution)/shard_map/attend/pallas_call | solution.py:378
  161.0 43.4 %give_back.1 = bf16[512,256]{1,0:T(8,128)(2,1)S(1)} custom-call(bf16[1024,256]{1,0:T(8,128)(2,1)S(1)} %attend.1.result_ref, s32[8,1024]{1,0:T(8,128)S(1)} %get-tuple-element.9.rank_ref, s32[8,512]{1,0:T(8,128)S(1)} %get-tuple-element.10.place_ref), custom_call_target="tpu_custom_call" | custom-call | tf_op jit(solution)/shard_map/give_back/pallas_call | solution.py:398
  204.4 0.7 copy.10
Async XLA Ops:
  0.0 0.9 copy-start.4
  1.0 0.7 copy-start.6
  39.1 2.0 copy-start
  41.1 1.0 copy-start.1
  42.1 1.0 copy-start.2
  43.2 1.0 copy-start.3
  44.2 0.9 copy-start.5
  45.1 0.7 copy-start.7
  45.8 0.7 copy-start.8

commit v2 on v1

--- a/solution.py
+++ b/solution.py
@@ -25,9 +25,16 @@
     return jnp.where(condition, 1.0, 0.0).astype(BF16)
 
 
+def normalize(values, gain):
+    mean = jnp.mean(values, axis=-1, keepdims=True)
+    centered = values - mean
+    variance = jnp.mean(centered * centered, axis=-1, keepdims=True)
+    return centered * lax.rsqrt(variance + 1e-05) * gain
+
+
 def route_kernel(
-    regions, loops, tokens_ref, dest_ref, pool_ref, place_ref, rank_ref,
-    outbox, inbox, packed, send_a, recv_a, send_g, recv_g, local_sem,
+    regions, loops, tokens_ref, dest_ref, gain1_ref, pool_ref, raw_ref, place_ref, rank_ref,
+    outbox, inbox, normed, packed, send_a, recv_a, send_g, recv_g, local_sem,
 ):
     rows, width = tokens_ref.shape
     chunk = CAP * loops
@@ -79,8 +86,15 @@
     own = pl.ds(pl.multiple_of(region * chunk, chunk), chunk)
     inbox[own, :] = outbox[own, :]
     earlier = one_hot(iota((slots, slots), 0) < iota((slots, slots), 1))
-    for copy in exchanges:
+
+    def norm_rows(at):
+        normed[at, :] = normalize(inbox[at, :].astype(F32), gain1_ref[...]).astype(BF16)
+
+    norm_rows(own)
+    for k, copy in zip(range(1, regions), exchanges):
         copy.wait_recv()
+        source = lax.rem(region + regions - k, regions)
+        norm_rows(pl.ds(pl.multiple_of(source * chunk, chunk), chunk))
 
     alive = jnp.where(inbox[:, :128].astype(F32) < 8.0, 1.0, 0.0)
     alive_row = alive.T[:16, :]
@@ -89,7 +103,7 @@
     rank_ref[...] = slot[:8, :]
     squeeze = one_hot(iota((slots, slots), 0) == slot[0:1, :])
     packed[pl.ds(0, slots), :] = jnp.dot(
-        squeeze, inbox[...], preferred_element_type=F32
+        squeeze, normed[...], preferred_element_type=F32
     ).astype(BF16)
     count = jnp.sum(alive_row, axis=1, keepdims=True)
     high = jnp.floor(count * (1.0 / 128.0))
@@ -121,6 +135,7 @@
     ]
     keep = pltpu.make_async_copy(packed, pool_ref.at[loop], local_sem)
     keep.start()
+    raw_ref[...] = jnp.dot(squeeze, inbox[...], preferred_element_type=F32).astype(BF16)
     started[0].wait_recv()
     started.append(move(5, pool_ref.at[left], left, half0, right))
     started.append(move(6, pool_ref.at[left], left, half0, sibling))
@@ -142,90 +157,94 @@
     keep.wait()
 
 
-def normalize(values, gain):
-    mean = jnp.mean(values, axis=-1, keepdims=True)
-    centered = values - mean
-    variance = jnp.mean(centered * centered, axis=-1, keepdims=True)
-    return centered * lax.rsqrt(variance + 1e-05) * gain
-
-
 def attend_kernel(
-    slots, tq, big, small,
-    pool_ref, gain1_ref, wqkv_ref, wout_ref, gain2_ref, whid_ref, wback_ref, out_ref,
-    keys, vals_a, vals_b, stacked, accum, top, key_norm,
+    slots, tq, tail_tq, big, small,
+    pool_ref, raw_ref, wqkv_hbm, wout_hbm, gain2_ref, whid_hbm, wback_hbm, out_ref,
+    pool, raw, wqkv_ref, wout_ref, whid_ref, wback_ref,
+    keys, vals_a, vals_b, stacked, accum, top, key_top, sems,
 ):
-    loops = pool_ref.shape[0]
-    width = gain1_ref.shape[1]
+    loops, width = pool_ref.shape[0], pool_ref.shape[2]
     head = width // HEADS
     kt = min(256, slots)
     scale = math.log2(math.e) / math.sqrt(head)
     me = lax.axis_index("loop")
-    gain1, gain2 = gain1_ref[...], gain2_ref[...]
+
+    loads = [
+        pltpu.make_async_copy(src, dst, sems.at[n])
+        for n, (src, dst) in enumerate(
+            [(wqkv_hbm, wqkv_ref)]
+            + [(pool_ref.at[j], pool.at[j]) for j in range(loops)]
+            + [(raw_ref, raw), (wout_hbm, wout_ref), (whid_hbm, whid_ref), (wback_hbm, wback_ref)]
+        )
+    ]
+    for load in loads:
+        load.start()
+    out_ref[...] = jnp.zeros_like(out_ref)
+    key_top[...] = jnp.zeros_like(key_top)
+    loads[0].wait()
 
     def even_lane(shape):
         return lax.rem(iota(shape, 1) // head, 2) == 0
 
     def live_rows(j):
-        note = pool_ref[j, pl.ds(slots, EXTRA), :].astype(F32)
+        note = pool[j, pl.ds(slots, EXTRA), :].astype(F32)
         high, low = jnp.max(note[:, :128]), jnp.max(note[:, 128:])
         return (high * 128.0 + low).astype(jnp.int32)
 
-    to_head = one_hot(iota((width, 128), 0) // head == iota((width, 128), 1))
-    key_norm[...] = jnp.zeros_like(key_norm)
-
-    def project(j, base):
+    base = jnp.int32(0)
+    even = even_lane((kt, width))
+    for j in range(loops):
+        loads[1 + j].wait()
         count = live_rows(j)
 
-        def tile(t, carry):
+        def tile(t, carry, j=j, base=base, count=count):
             start = pl.multiple_of(t * kt, kt)
-            x = pool_ref[j, pl.ds(start, kt), :].astype(F32)
-            normed = normalize(x, gain1).astype(BF16)
-            kv = jnp.dot(normed, wqkv_ref[:, width:], preferred_element_type=F32)
-            k = kv[:, :width].astype(BF16)
+            kv = jnp.dot(
+                pool[j, pl.ds(start, kt), :], wqkv_ref[:, width:], preferred_element_type=F32
+            )
+            k = kv[:, :width]
             v = kv[:, width:]
             valid = iota((kt, width), 0) + start < count
-            even = even_lane((kt, width))
             at = pl.ds(pl.multiple_of(base + start, 16), kt)
-            keys[at, :] = k
+            keys[at, :] = k.astype(BF16)
             vals_a[at, :] = jnp.where(valid, jnp.where(even, v, 1.0), 0.0).astype(BF16)
             vals_b[at, :] = jnp.where(valid, jnp.where(even, 1.0, v), 0.0).astype(BF16)
-            square = k.astype(F32)
-            norms = jnp.dot((square * square).astype(BF16), to_head, preferred_element_type=F32)
-            key_norm[...] = jnp.maximum(
-                key_norm[...], jnp.max(norms.reshape(kt // 8, 8, 128), axis=0)
-            )
+            peak = jnp.max(jnp.abs(k).reshape(kt // 8, 8, width), axis=0)
+            key_top[...] = jnp.maximum(key_top[...], peak)
             return carry
 
         lax.fori_loop(0, pl.cdiv(count, kt), tile, 0)
-        return base + pl.cdiv(count, 16) * 16
-
-    total_rows = lax.fori_loop(0, loops, project, jnp.int32(0))
+        base = base + pl.cdiv(count, 16) * 16
+
+    total_rows = base
     tail = pl.ds(pl.multiple_of(total_rows, 16), small)
     for ref in (keys, vals_a, vals_b):
         ref[tail, :] = jnp.zeros((small, width), BF16)
-    key_top = jnp.max(key_norm[...], axis=0, keepdims=True)
+    highest = jnp.max(key_top[...], axis=0, keepdims=True)
     small_count = pl.cdiv(total_rows, small)
     big_count = small_count // (big // small)
     small_first = big_count * (big // small)
-
-    out_ref[...] = jnp.zeros_like(out_ref)
+    for load in loads[1 + loops :]:
+        load.wait()
+
     mine = live_rows(me)
+    to_head = one_hot(iota((width, 128), 0) // head == iota((width, 128), 1))
     flag_lane = one_hot(iota((8, width), 1) == head)
     order = tuple(range(0, HEADS, 2)) + tuple(range(1, HEADS, 2))
-    group = HEADS // 2 * tq
-
-    def queries(i, carry):
-        start = pl.multiple_of(i * tq, tq)
-        x = pool_ref[me, pl.ds(start, tq), :].astype(F32)
-        normed = normalize(x, gain1).astype(BF16)
-        q = jnp.dot(normed, wqkv_ref[:, :width], preferred_element_type=F32).astype(BF16)
+
+    def queries(tq, start):
+        group = HEADS // 2 * tq
+        at_q = pl.ds(start, tq)
+        q = jnp.dot(
+            pool[me, at_q, :], wqkv_ref[:, :width], preferred_element_type=F32
+        ).astype(BF16)
         lane_head = iota((tq, width), 1) // head
         for n, h in enumerate(order):
             stacked[n * tq : (n + 1) * tq, :] = jnp.where(lane_head == h, q, jnp.zeros_like(q))
-        square = q.astype(F32)
-        norms = jnp.dot((square * square).astype(BF16), to_head, preferred_element_type=F32)
-        bound = jnp.max(jnp.max(norms, axis=0, keepdims=True) * key_top)
-        accum[...] = jnp.zeros_like(accum)
+        reach = (jnp.abs(q.astype(F32)) * highest).astype(BF16)
+        bound = jnp.max(jnp.dot(reach, to_head, preferred_element_type=F32))
+        accum[: 2 * group, :] = jnp.zeros((2 * group, width), F32)
+        halves = ((slice(0, group), vals_a), (slice(group, 2 * group), vals_b))
 
         def scores(at, rows):
             return scale * lax.dot_general(
@@ -235,10 +254,7 @@
         def plain(size, first):
             def step(j, carry):
                 at = pl.ds(pl.multiple_of((first + j) * size, size), size)
-                for rows, vals in (
-                    (slice(0, group), vals_a),
-                    (slice(group, 2 * group), vals_b),
-                ):
+                for rows, vals in halves:
                     weights = jnp.exp2(scores(at, rows)).astype(BF16)
                     accum[rows, :] += jnp.dot(weights, vals[at, :], preferred_element_type=F32)
                 return carry
@@ -251,7 +267,7 @@
                 flag_lane, vals_a[at, :], (((1,), (1,)), ((), ())), preferred_element_type=F32
             )
             live = flags[0:1, :] > 0.5
-            for rows, vals in ((slice(0, group), vals_a), (slice(group, 2 * group), vals_b)):
+            for rows, vals in halves:
                 values = jnp.where(live, scores(at, rows), -1e30)
                 old = top[rows, :]
                 new = jnp.maximum(old, jnp.max(values, axis=1, keepdims=True))
@@ -263,7 +279,7 @@
                 )
             return carry
 
-        unshifted = bound * (1.05 * scale * scale) < 4096.0
+        unshifted = bound * (1.02 * scale) < 90.0
 
         @pl.when(unshifted)
         def _():
@@ -272,7 +288,7 @@
 
         @pl.when(jnp.logical_not(unshifted))
         def _():
-            top[...] = jnp.full(top.shape, -1e30, F32)
+            top[: 2 * group, :] = jnp.full((2 * group, 128), -1e30, F32)
             lax.fori_loop(0, small_count, shifted, 0)
 
         part_a = jnp.zeros((tq, width), F32)
@@ -288,15 +304,29 @@
             even, pltpu.roll(sums, width - head, 1), pltpu.roll(sums, head, 1)
         )
         attended = (numerator / total).astype(BF16)
-        mixed = x + jnp.dot(attended, wout_ref[...], preferred_element_type=F32)
-        normed2 = normalize(mixed, gain2).astype(BF16)
+        mixed = raw[at_q, :].astype(F32) + jnp.dot(
+            attended, wout_ref[...], preferred_element_type=F32
+        )
+        normed2 = normalize(mixed, gain2_ref[...]).astype(BF16)
         inner = jnp.dot(normed2, whid_ref[...], preferred_element_type=F32)
         hidden = (0.5 * inner * (1.0 + lax.erf(inner * math.sqrt(0.5)))).astype(BF16)
         result = mixed + jnp.dot(hidden, wback_ref[...], preferred_element_type=F32)
-        out_ref[pl.ds(start, tq), :] = result.astype(BF16)
+        out_ref[at_q, :] = result.astype(BF16)
+
+    parts = pl.cdiv(mine, tail_tq)
+    per_tile = tq // tail_tq
+    full = parts // per_tile
+
+    def full_tile(i, carry):
+        queries(tq, pl.multiple_of(i * tq, tq))
         return carry
 
-    lax.fori_loop(0, pl.cdiv(mine, tq), queries, 0)
+    lax.fori_loop(0, full, full_tile, 0)
+    for rest in range(1, per_tile):
+
+        @pl.when(parts - full * per_tile == rest)
+        def _(rest=rest):
+            queries(rest * tail_tq, pl.multiple_of(full * tq, tq))
 
 
 def give_back_kernel(
@@ -345,23 +375,29 @@
         copy.wait_send()
 
 
-def local(tq, big, small, tokens, dest, norm1_gain, w_qkv, w_out, norm2_gain, w_hidden, w_back):
+def local(
+    tiles, tokens, dest, norm1_gain, w_qkv, w_out, norm2_gain, w_hidden, w_back
+):
+    tq, tail_tq, big, small = tiles
     rows, width = tokens.shape
     regions, loops = lax.axis_size("region"), lax.axis_size("loop")
     chunk = CAP * loops
     slots = regions * chunk
     vmem = pl.BlockSpec(memory_space=pltpu.VMEM)
-    params = functools.partial(pltpu.CompilerParams, vmem_limit_bytes=48 * 1024 * 1024)
-    pool, place, rank = pl.pallas_call(
+    hbm = pl.BlockSpec(memory_space=pltpu.HBM)
+    params = functools.partial(pltpu.CompilerParams, vmem_limit_bytes=62 * 1024 * 1024)
+    pool, raw, place, rank = pl.pallas_call(
         functools.partial(route_kernel, regions, loops),
         out_shape=(
             jax.ShapeDtypeStruct((loops, slots + EXTRA, width), BF16),
+            jax.ShapeDtypeStruct((slots, width), BF16),
             jax.ShapeDtypeStruct((8, rows), jnp.int32),
             jax.ShapeDtypeStruct((8, slots), jnp.int32),
         ),
-        in_specs=[vmem] * 2,
-        out_specs=(pl.BlockSpec(memory_space=pl.ANY), vmem, vmem),
+        in_specs=[vmem] * 3,
+        out_specs=(hbm, vmem, vmem, vmem),
         scratch_shapes=[
+            pltpu.VMEM((slots, width), BF16),
             pltpu.VMEM((slots, width), BF16),
             pltpu.VMEM((slots, width), BF16),
             pltpu.VMEM((slots + EXTRA, width), BF16),
@@ -373,28 +409,32 @@
         ],
         compiler_params=params(collective_id=0, has_side_effects=True),
         name="route",
-    )(tokens, dest.reshape(1, rows))
+    )(tokens, dest.reshape(1, rows), norm1_gain.reshape(1, width))
     key_rows = loops * slots + small + min(256, slots)
     result = pl.pallas_call(
-        functools.partial(attend_kernel, slots, tq, big, small),
+        functools.partial(attend_kernel, slots, *tiles),
         out_shape=jax.ShapeDtypeStruct((slots, width), BF16),
-        in_specs=[vmem] * 7,
+        in_specs=[hbm, hbm, hbm, hbm, vmem, hbm, hbm],
         out_specs=vmem,
         scratch_shapes=[
+            pltpu.VMEM((loops, slots + EXTRA, width), BF16),
+            pltpu.VMEM((slots, width), BF16),
+            pltpu.VMEM(w_qkv.shape, BF16),
+            pltpu.VMEM(w_out.shape, BF16),
+            pltpu.VMEM(w_hidden.shape, BF16),
+            pltpu.VMEM(w_back.shape, BF16),
             pltpu.VMEM((key_rows, width), BF16),
             pltpu.VMEM((key_rows, width), BF16),
             pltpu.VMEM((key_rows, width), BF16),
             pltpu.VMEM((HEADS * tq, width), BF16),
             pltpu.VMEM((HEADS * tq, width), F32),
             pltpu.VMEM((HEADS * tq, 128), F32),
-            pltpu.VMEM((8, 128), F32),
+            pltpu.VMEM((8, width), F32),
+            pltpu.SemaphoreType.DMA((loops + 5,)),
         ],
         compiler_params=params(),
         name="attend",
-    )(
-        pool, norm1_gain.reshape(1, width), w_qkv, w_out, norm2_gain.reshape(1, width),
-        w_hidden, w_back,
-    )
+    )(pool, raw, w_qkv, w_out, norm2_gain.reshape(1, width), w_hidden, w_back)
     return pl.pallas_call(
         functools.partial(give_back_kernel, regions, loops),
         out_shape=jax.ShapeDtypeStruct((rows, width), BF16),
@@ -411,10 +451,10 @@
     )(result, rank, place)
 
 
-def build(mesh, tq, big, small):
+def build(mesh, tiles):
     spread = P(("region", "loop"), None)
     return jax.shard_map(
-        functools.partial(local, tq, big, small),
+        functools.partial(local, tiles),
         mesh=mesh,
         in_specs=(spread, spread) + (P(),) * 6,
         out_specs=spread,
@@ -423,4 +463,4 @@
 
 
 def solution(mesh):
-    return build(mesh, 256, 2048, 512)
+    return build(mesh, (256, 128, 2048, 512))

time: 205 us -> 185 us (0.902)
  Pallas kernels: 195 us -> 183 us
  local copies, waits for them, and re-layouts: 9.63 us -> 1.67 us
    pallas_call x1, Pallas kernels: 115 us -> 101 us  [local(): pl.pallas_call(functools.partial(attend_kernel, slots, *tiles), out_shape...]
    unnamed x19 -> x1, local copies, waits for them, and re-layouts: 9.63 us -> 1.67 us
    pallas_call x1, Pallas kernels: 37.5 us -> 41.2 us  [local(): pl.pallas_call(functools.partial(route_kernel, regions, loops), out_shape...]
where the time goes in v2:
time: 185 us
  Pallas kernels  183 us (99%)
    pallas_call x1, Pallas kernels, local(): pl.pallas_call(functools.partial(attend_kernel, slots, *tiles), out_shape...  101 us
    pallas_call x1, Pallas kernels, local(): pl.pallas_call(functools.partial(give_back_kernel, regions, loops), out_s...  41.5 us
    pallas_call x1, Pallas kernels, local(): pl.pallas_call(functools.partial(route_kernel, regions, loops), out_shape...  41.2 us

profile of v2, /device:TPU:1, one launch (start us, length us, event | category | flops | bytes accessed | tf_op | source)
XLA Modules:
  0.0 185.1 jit_solution(1330858428096225910)
XLA Ops:
  0.0 41.2 %route.1 = (bf16[8,1040,256]{2,1,0:T(8,128)(2,1)}, bf16[1024,256]{1,0:T(8,128)(2,1)}, s32[8,512]{1,0:T(8,128)}, s32[8,1024]{1,0:T(8,128)}) custom-call(bf16[512,256]{1,0:T(8,128)(2,1)} %tokens_ref.1, s32[1,512]{1,0:T(1,128)} %bitcast.3, f32[1,256]{1,0:T(1,128)} %bitcast.4), custom_call_target="tpu_custom_call" | custom-call | tf_op jit(solution)/shard_map/route/pallas_call | solution.py:389
  41.3 100.7 %attend.1.result_ref = bf16[1024,256]{1,0:T(8,128)(2,1)} custom-call(bf16[8,1040,256]{2,1,0:T(8,128)(2,1)} %get-tuple-element.9.pool_ref, bf16[1024,256]{1,0:T(8,128)(2,1)} %get-tuple-element.10.raw_ref, bf16[256,768]{1,0:T(8,128)(2,1)} %wqkv_hbm.1, bf16[256,256]{1,0:T(8,128)(2,1)} %wout_hbm.1, f32[1,256]{1,0:T(1,128)} %bitcast.5, ...), custom_call_target="tpu_custom_call" | custom-call | tf_op jit(solution)/shard_map/attend/pallas_call | solution.py:414
  141.9 41.5 %give_back.1 = bf16[512,256]{1,0:T(8,128)(2,1)} custom-call(bf16[1024,256]{1,0:T(8,128)(2,1)} %attend.1.result_ref, s32[8,1024]{1,0:T(8,128)} %get-tuple-element.11.rank_ref, s32[8,512]{1,0:T(8,128)} %get-tuple-element.12.place_ref), custom_call_target="tpu_custom_call" | custom-call | tf_op jit(solution)/shard_map/give_back/pallas_call | solution.py:438
  183.4 1.7 copy.10

commit v3 on v2

v3 whole, which is shorter than its diff:
```python
import functools
import math

import jax
import jax.numpy as jnp
from jax import lax
from jax.experimental import pallas as pl
from jax.experimental.pallas import tpu as pltpu
from jax.sharding import PartitionSpec as P

HEADS = 8
CAP = 8
MARK = 16.0
MESH = pl.DeviceIdType.MESH
EXTRA = 16
F32 = jnp.float32
BF16 = jnp.bfloat16


def iota(shape, dim):
    return lax.broadcasted_iota(jnp.int32, shape, dim)


def one_hot(condition):
    return jnp.where(condition, 1.0, 0.0).astype(BF16)


def normalize(values, gain):
    mean = jnp.mean(values, axis=-1, keepdims=True)
    centered = values - mean
    variance = jnp.mean(centered * centered, axis=-1, keepdims=True)
    return centered * lax.rsqrt(variance + 1e-05) * gain


def head_order():
    return tuple(range(0, HEADS, 2)) + tuple(range(1, HEADS, 2))


def even_lane(shape, head):
    return lax.rem(iota(shape, 1) // head, 2) == 0


def project(rows, w_kv, valid, width):
    kv = jnp.dot(rows, w_kv, preferred_element_type=F32)
    k, v = kv[:, :width], kv[:, width:]
    even = even_lane(v.shape, width // HEADS)
    with_odd = jnp.where(valid, jnp.where(even, v, 1.0), 0.0).astype(BF16)
    with_even = jnp.where(valid, jnp.where(even, 1.0, v), 0.0).astype(BF16)
    peak = jnp.max(jnp.abs(k).reshape(k.shape[0] // 8, 8, width), axis=0)
    return k.astype(BF16), with_odd, with_even, peak


def collect(block, tq, width):
    group = HEADS // 2 * tq
    pair = iota((tq, width), 1) // (2 * (width // HEADS))
    part_a = jnp.zeros((tq, width), F32)
    part_b = jnp.zeros((tq, width), F32)
    for n in range(HEADS // 2):
        part_a = jnp.where(pair == n, block[n * tq : (n + 1) * tq, :], part_a)
        part_b = jnp.where(pair == n, block[group + n * tq : group + (n + 1) * tq, :], part_b)
    even = even_lane((tq, width), width // HEADS)
    return jnp.where(even, part_a, part_b), jnp.where(even, part_b, part_a)


def route_kernel(
    regions, loops, tq, tokens_ref, dest_ref, gain1_ref, wqkv_ref,
    late_ref, first_keys, first_a, first_b, query_ref, raw_ref, note_ref, num_ref, sum_ref,
    key_top, place_ref, rank_ref,
    outbox, inbox, normed, pool, own_late, keys, vals, stacked, accum,
    send_a, recv_a, send_g, recv_g, local_sem,
):
    rows, width = tokens_ref.shape
    chunk = CAP * loops
    slots = regions * chunk
    half = slots // 2
    chips = loops // 2
    head = width // HEADS
    scale = math.log2(math.e) / math.sqrt(head)
    region, loop = lax.axis_index("region"), lax.axis_index("loop")
    chip, core = loop // 2, lax.rem(loop, 2)
    sibling = chip * 2 + (1 - core)
    right_chip, left_chip = lax.rem(chip + 1, chips), lax.rem(chip + chips - 1, chips)
    far_chip = lax.rem(chip + 2, chips)
    right, left, far = right_chip * 2 + core, left_chip * 2 + core, far_chip * 2 + core

    barrier = pltpu.get_barrier_semaphore()
    for k in range(1, regions):
        pl.semaphore_signal(
            barrier, inc=1, device_id=(lax.rem(region + k, regions), loop), device_id_type=MESH
        )
    for peer in (sibling, left, right):
        pl.semaphore_signal(barrier, inc=1, device_id=(region, peer), device_id_type=MESH)

    owner_region = dest_ref[...] // loops
    hot = one_hot(owner_region == iota((regions, rows), 0))
    upper = one_hot(iota((rows, rows), 0) <= iota((rows, rows), 1))
    before = jnp.dot(hot, upper, preferred_element_type=F32)
    rank = jnp.sum(before * hot.astype(F32), axis=0, keepdims=True).astype(jnp.int32) - 1
    place = owner_region * chunk + rank
    place_ref[...] = jnp.broadcast_to(place, place_ref.shape)
    spread = one_hot(iota((slots, rows), 0) == place)
    sorted_rows = jnp.dot(spread, tokens_ref[...], preferred_element_type=F32)
    held = jnp.dot(spread, jnp.ones((rows, width), BF16), preferred_element_type=F32)
    outbox[...] = (sorted_rows + (1.0 - held) * MARK).astype(BF16)

    pl.semaphore_wait(barrier, regions - 1 + 3)

    def exchange(k):
        peer = lax.rem(region + k, regions)
        return pltpu.make_async_remote_copy(
            src_ref=outbox.at[pl.ds(pl.multiple_of(peer * chunk, chunk), chunk)],
            dst_ref=inbox.at[pl.ds(pl.multiple_of(region * chunk, chunk), chunk)],
            send_sem=send_a.at[k],
            recv_sem=recv_a.at[k],
            device_id=(peer, loop),
            device_id_type=MESH,
        )

    exchanges = [exchange(k) for k in range(1, regions)]
    for copy in exchanges:
        copy.start()
    own = pl.ds(pl.multiple_of(region * chunk, chunk), chunk)
    inbox[own, :] = outbox[own, :]
    earlier = one_hot(iota((slots, slots), 0) < iota((slots, slots), 1))

    def norm_rows(at):
        normed[at, :] = normalize(inbox[at, :].astype(F32), gain1_ref[...]).astype(BF16)

    norm_rows(own)
    for k, copy in zip(range(1, regions), exchanges):
        copy.wait_recv()
        source = lax.rem(region + regions - k, regions)
        norm_rows(pl.ds(pl.multiple_of(source * chunk, chunk), chunk))

    alive = jnp.where(inbox[:, :128].astype(F32) < 8.0, 1.0, 0.0)
    alive_row = alive.T[:16, :]
    ahead = jnp.dot(alive_row.astype(BF16), earlier, preferred_element_type=F32)
    slot = jnp.where(alive_row > 0.0, ahead, -1.0).astype(jnp.int32)
    rank_ref[...] = slot[:8, :]
    squeeze = one_hot(iota((slots, slots), 0) == slot[0:1, :])
    packed = jnp.dot(squeeze, normed[...], preferred_element_type=F32).astype(BF16)
    count = jnp.sum(alive_row, axis=1, keepdims=True)
    high = jnp.floor(count * (1.0 / 128.0))
    pool[loop, pl.ds(0, EXTRA), :] = jnp.where(
        iota((EXTRA, width), 1) < 128, high, count - 128.0 * high
    ).astype(BF16)
    pool[loop, pl.ds(EXTRA, half), :] = packed[:half, :]
    own_late[...] = packed[half:, :]

    def move(n, src, dst, peer):
        return pltpu.make_async_remote_copy(
            src_ref=src,
            dst_ref=dst,
            send_sem=send_g.at[n],
            recv_sem=recv_g.at[n],
            device_id=(region, peer),
            device_id_type=MESH,
        )

    def early(n, index, peer):
        return move(n, pool.at[index], pool.at[index], peer)

    def late(n, index, peer):
        return move(n, late_ref.at[index], late_ref.at[index], peer)

    moves = [
        early(0, loop, right),
        early(1, loop, left),
        early(2, loop, sibling),
        move(3, own_late, late_ref.at[loop], right),
        move(4, own_late, late_ref.at[loop], left),
        move(5, own_late, late_ref.at[loop], sibling),
        early(6, left, right),
        early(7, left, sibling),
        early(8, right, sibling),
        late(9, right, left),
        late(10, right, sibling),
        late(11, left, sibling),
        early(12, far, sibling),
        late(13, far, sibling),
    ]
    for n in range(6):
        moves[n].start()
    keep = pltpu.make_async_copy(own_late, late_ref.at[loop], local_sem.at[0])
    keep.start()

    own_rows = jnp.concatenate([pool[loop, pl.ds(EXTRA, half), :], own_late[...]], axis=0)
    q_all = jnp.dot(own_rows, wqkv_ref[:, :width], preferred_element_type=F32).astype(BF16)
    query_ref[...] = q_all
    tiles = half // tq
    lane_head = iota((tq, width), 1) // head
    for t in range(tiles):
        q = q_all[t * tq : (t + 1) * tq, :]
        for n, h in enumerate(head_order()):
            stacked[t, n * tq : (n + 1) * tq, :] = jnp.where(lane_head == h, q, jnp.zeros_like(q))
    raw_ref[...] = jnp.dot(squeeze, inbox[...], preferred_element_type=F32).astype(BF16)
    accum[...] = jnp.zeros_like(accum)
    key_top[...] = jnp.zeros_like(key_top)

    group = HEADS // 2 * tq

    def hand_over(p):
        at = pl.ds(pl.multiple_of(2 * p * half, 2 * half), 2 * half)
        return [
            pltpu.make_async_copy(src.at[at], dst.at[at], local_sem.at[1 + 3 * p + n])
            for n, (src, dst) in enumerate(
                ((keys, first_keys), (vals.at[0], first_a), (vals.at[1], first_b))
            )
        ]

    def prepare(p):
        turn = jnp.where(p == 1, chips - 1, jnp.where(p == 2, 1, jnp.where(p == 3, 2, 0)))

        def one(c, carry):
            j = lax.rem(chip + turn, chips) * 2 + lax.rem(core + c, 2)
            note = pool[j, pl.ds(0, EXTRA), :]
            note_ref[j] = note
            note = note.astype(F32)
            live = note[0:1, 0:1] * 128.0 + note[0:1, 128:129]
            valid = iota((half, width), 0).astype(F32) < live
            k, va, vb, peak = project(
                pool[j, pl.ds(EXTRA, half), :], wqkv_ref[:, width:], valid, width
            )
            at = pl.ds(pl.multiple_of((2 * p + c) * half, half), half)
            keys[at, :] = k
            vals[0, at, :] = va
            vals[1, at, :] = vb
            key_top[...] = jnp.maximum(key_top[...], peak)
            return carry

        lax.fori_loop(0, 2, one, 0)
        for copy in hand_over(p):
            copy.start()

    script = {
        0: ["w2"],
        tiles: ["w0", "s6", "s7", "w1", "s8", "w7"],
        tiles + tiles // 2: ["w4", "s9", "s10", "w3", "s11"],
        2 * tiles: ["w8"],
        3 * tiles: ["w6", "s12", "w9", "s13", "w12"],
    }

    def advance(step, carry):
        p, tile = step // tiles, lax.rem(step, tiles)
        for when, acts in script.items():

            @pl.when(step == when)
            def _(acts=acts):
                for act in acts:
                    copy = moves[int(act[1:])]
                    if act[0] == "w":
                        copy.wait_recv()
                    else:
                        copy.start()

        @pl.when(tile == 0)
        def _():
            prepare(p)

        at = pl.ds(pl.multiple_of(2 * p * half, 2 * half), 2 * half)

        def part(side, carry):
            lines = pl.ds(pl.multiple_of(side * group, group), group)
            scores = scale * lax.dot_general(
                stacked[tile, lines, :], keys[at, :], (((1,), (1,)), ((), ())),
                preferred_element_type=F32,
            )
            weights = jnp.exp2(scores).astype(BF16)
            accum[tile, lines, :] += jnp.dot(
                weights, vals[side, at, :], preferred_element_type=F32
            )
            return carry

        return lax.fori_loop(0, 2, part, carry)

    lax.fori_loop(0, 4 * tiles, advance, 0)
    for t in range(tiles):
        numerator, sums = collect(accum[t], tq, width)
        num_ref[t * tq : (t + 1) * tq, :] = numerator
        sum_ref[t * tq : (t + 1) * tq, :] = sums
    for n in (5, 10, 11, 13):
        moves[n].wait_recv()
    for copy in exchanges + moves:
        copy.wait_send()
    keep.wait()
    for p in range(4):
        for copy in hand_over(p):
            copy.wait()


def attend_kernel(
    tq, big, small,
    late_hbm, first_keys, first_a, first_b, query_hbm, raw_hbm, num_hbm, sum_hbm, wqkv_hbm,
    wout_hbm, whid_hbm, wback_hbm, note_ref, first_top, gain2_ref, out_ref,
    late, query, raw, num, sums_in, wkv, wout, whid, wback,
    keys, vals_a, vals_b, stacked, accum, top, key_top, sems,
):
    loops, half, width = late_hbm.shape
    slots = query_hbm.shape[0]
    head = width // HEADS
    kt = min(256, half)
    early_rows = loops * half
    scale = math.log2(math.e) / math.sqrt(head)
    me = lax.axis_index("loop")

    pairs = [(wqkv_hbm.at[:, pl.ds(width, 2 * width)], wkv)]
    pairs += [(late_hbm.at[j], late.at[j]) for j in range(loops)]
    pairs += [(query_hbm, query), (raw_hbm, raw), (num_hbm, num), (sum_hbm, sums_in)]
    pairs += [(wout_hbm, wout), (whid_hbm, whid), (wback_hbm, wback)]
    front = pl.ds(0, early_rows)
    pairs += [
        (first_keys, keys.at[front]), (first_a, vals_a.at[front]), (first_b, vals_b.at[front]),
    ]
    loads = [pltpu.make_async_copy(src, dst, sems.at[n]) for n, (src, dst) in enumerate(pairs)]
    for load in loads:
        load.start()
    out_ref[...] = jnp.zeros_like(out_ref)
    key_top[...] = first_top[...]

    def live_rows(j):
        note = note_ref[j].astype(F32)
        high, low = jnp.max(note[:, :128]), jnp.max(note[:, 128:])
        return (high * 128.0 + low).astype(jnp.int32)

    counts = [live_rows(j) for j in range(loops)]
    loads[0].wait()
    base = jnp.int32(early_rows)
    for j in range(loops):
        loads[1 + j].wait()
        count = jnp.maximum(counts[j] - half, 0)

        def tile(t, carry, j=j, base=base, count=count):
            start = pl.multiple_of(t * kt, kt)
            valid = iota((kt, width), 0) + start < count
            k, va, vb, peak = project(late[j, pl.ds(start, kt), :], wkv[...], valid, width)
            at = pl.ds(pl.multiple_of(base + start, 16), kt)
            keys[at, :] = k
            vals_a[at, :] = va
            vals_b[at, :] = vb
            key_top[...] = jnp.maximum(key_top[...], peak)
            return carry

        lax.fori_loop(0, pl.cdiv(count, kt), tile, 0)
        base = base + pl.cdiv(count, 16) * 16

    total_rows = base
    tail = pl.ds(pl.multiple_of(total_rows, 16), small)
    for ref in (keys, vals_a, vals_b):
        ref[tail, :] = jnp.zeros((small, width), BF16)
    highest = jnp.max(key_top[...], axis=0, keepdims=True)
    for load in loads[1 + loops : -3]:
        load.wait()

    mine = live_rows(me)
    to_head = one_hot(iota((width, 128), 0) // head == iota((width, 128), 1))
    flag_lane = one_hot(iota((8, width), 1) == head)
    reach = (jnp.abs(query[...].astype(F32)) * highest).astype(BF16)
    bound = jnp.max(jnp.dot(reach, to_head, preferred_element_type=F32))
    unshifted = bound * (1.02 * scale) < 90.0

    def wait_early(condition):
        @pl.when(condition)
        def _():
            for load in loads[-3:]:
                load.wait()

    wait_early(jnp.logical_not(unshifted))

    def queries(tq, start):
        group = HEADS // 2 * tq
        at_q = pl.ds(start, tq)
        q = query[at_q, :]
        lane_head = iota((tq, width), 1) // head
        for n, h in enumerate(head_order()):
            stacked[n * tq : (n + 1) * tq, :] = jnp.where(lane_head == h, q, jnp.zeros_like(q))
        accum[: 2 * group, :] = jnp.zeros((2 * group, width), F32)
        halves = ((slice(0, group), vals_a), (slice(group, 2 * group), vals_b))
        begun = jnp.logical_and(unshifted, start < half)
        first = jnp.where(begun, early_rows, 0)
        blocks = pl.cdiv(total_rows - first, small)

        def scores(at, rows):
            return scale * lax.dot_general(
                stacked[rows, :], keys[at, :], (((1,), (1,)), ((), ())), preferred_element_type=F32
            )

        def plain(size, offset):
            at = pl.ds(pl.multiple_of(offset, 16), size)
            for rows, vals in halves:
                weights = jnp.exp2(scores(at, rows)).astype(BF16)
                accum[rows, :] += jnp.dot(weights, vals[at, :], preferred_element_type=F32)

        def shifted(j, carry):
            at = pl.ds(pl.multiple_of(j * small, small), small)
            flags = lax.dot_general(
                flag_lane, vals_a[at, :], (((1,), (1,)), ((), ())), preferred_element_type=F32
            )
            live = flags[0:1, :] > 0.5
            for rows, vals in halves:
                values = jnp.where(live, scores(at, rows), -1e30)
                old = top[rows, :]
                new = jnp.maximum(old, jnp.max(values, axis=1, keepdims=True))
                top[rows, :] = new
                factor = jnp.exp2(old - new)
                weights = jnp.exp2(values - new[:, :1]).astype(BF16)
                accum[rows, :] = accum[rows, :] * factor[:, :1] + jnp.dot(
                    weights, vals[at, :], preferred_element_type=F32
                )
            return carry

        @pl.when(unshifted)
        def _():
            per = big // small
            many = blocks // per

            def step(j, carry):
                plain(big, first + j * big)
                return carry

            lax.fori_loop(0, many, step, 0)
            left = blocks - many * per
            offset = first + many * big
            size = big // 2
            while size >= small:
                units = size // small
                taken = left >= units

                @pl.when(taken)
                def _(size=size, offset=offset):
                    plain(size, offset)

                left = jnp.where(taken, left - units, left)
                offset = jnp.where(taken, offset + size, offset)
                size //= 2

        @pl.when(jnp.logical_not(unshifted))
        def _():
            top[: 2 * group, :] = jnp.full((2 * group, 128), -1e30, F32)
            lax.fori_loop(0, blocks, shifted, 0)

        numerator, sums = collect(accum[: 2 * group, :], tq, width)
        at_p = pl.ds(pl.multiple_of(jnp.where(start < half, start, 0), 16), tq)
        numerator = numerator + jnp.where(begun, num[at_p, :], 0.0)
        sums = sums + jnp.where(begun, sums_in[at_p, :], 0.0)
        even = even_lane((tq, width), head)
        total = jnp.where(
            even, pltpu.roll(sums, width - head, 1), pltpu.roll(sums, head, 1)
        )
        attended = (numerator / total).astype(BF16)
        mixed = raw[at_q, :].astype(F32) + jnp.dot(
            attended, wout[...], preferred_element_type=F32
        )
        normed2 = normalize(mixed, gain2_ref[...]).astype(BF16)
        inner = jnp.dot(normed2, whid[...], preferred_element_type=F32)
        hidden = (0.5 * inner * (1.0 + lax.erf(inner * math.sqrt(0.5)))).astype(BF16)
        result = mixed + jnp.dot(hidden, wback[...], preferred_element_type=F32)
        out_ref[at_q, :] = result.astype(BF16)

    tiles = pl.cdiv(mine, tq)
    begun_tiles = half // tq

    def each_tile(i, carry):
        wait_early(jnp.logical_and(unshifted, i == begun_tiles))
        queries(tq, pl.multiple_of(i * tq, tq))
        return carry

    lax.fori_loop(0, tiles, each_tile, 0)
    wait_early(jnp.logical_and(unshifted, tiles <= begun_tiles))


def give_back_kernel(
    regions, loops, result_ref, rank_ref, place_ref, out_ref, outbox, inbox, send, recv
):
    rows = out_ref.shape[0]
    chunk = CAP * loops
    slots = regions * chunk
    region, loop = lax.axis_index("region"), lax.axis_index("loop")
    barrier = pltpu.get_barrier_semaphore()
    for k in range(1, regions):
        pl.semaphore_signal(
            barrier, inc=1, device_id=(lax.rem(region + k, regions), loop), device_id_type=MESH
        )

    def column(row_ref):
        size = row_ref.shape[1]
        row = jnp.broadcast_to(row_ref[0:1, :].astype(F32), (128, size))
        return row.T[:, 0:1].astype(jnp.int32)

    unpack = one_hot(column(rank_ref) == iota((slots, slots), 1))
    outbox[...] = jnp.dot(unpack, result_ref[...], preferred_element_type=F32).astype(BF16)
    pl.semaphore_wait(barrier, regions - 1)

    def exchange(k):
        peer = lax.rem(region + k, regions)
        return pltpu.make_async_remote_copy(
            src_ref=outbox.at[pl.ds(pl.multiple_of(peer * chunk, chunk), chunk)],
            dst_ref=inbox.at[pl.ds(pl.multiple_of(region * chunk, chunk), chunk)],
            send_sem=send.at[k],
            recv_sem=recv.at[k],
            device_id=(peer, loop),
            device_id_type=MESH,
        )

    exchanges = [exchange(k) for k in range(1, regions)]
    for copy in exchanges:
        copy.start()
    own = pl.ds(pl.multiple_of(region * chunk, chunk), chunk)
    inbox[own, :] = outbox[own, :]
    take = one_hot(column(place_ref) == iota((rows, slots), 1))
    for copy in exchanges:
        copy.wait_recv()
    out_ref[...] = jnp.dot(take, inbox[...], preferred_element_type=F32).astype(BF16)
    for copy in exchanges:
        copy.wait_send()


def local(
    tiles, tokens, dest, norm1_gain, w_qkv, w_out, norm2_gain, w_hidden, w_back
):
    tq, big, small = tiles
    rows, width = tokens.shape
    regions, loops = lax.axis_size("region"), lax.axis_size("loop")
    chunk = CAP * loops
    slots = regions * chunk
    half = slots // 2
    vmem = pl.BlockSpec(memory_space=pltpu.VMEM)
    hbm = pl.BlockSpec(memory_space=pltpu.HBM)
    params = functools.partial(pltpu.CompilerParams, vmem_limit_bytes=62 * 1024 * 1024)
    shape = jax.ShapeDtypeStruct
    (
        late, first_keys, first_a, first_b, query, raw, notes, num, sums, key_top, place, rank,
    ) = pl.pallas_call(
        functools.partial(route_kernel, regions, loops, tq),
        out_shape=(
            shape((loops, half, width), BF16),
            shape((loops * half, width), BF16),
            shape((loops * half, width), BF16),
            shape((loops * half, width), BF16),
            shape((slots, width), BF16),
            shape((slots, width), BF16),
            shape((loops, EXTRA, width), BF16),
            shape((half, width), F32),
            shape((half, width), F32),
            shape((8, width), F32),
            shape((8, rows), jnp.int32),
            shape((8, slots), jnp.int32),
        ),
        in_specs=[vmem] * 4,
        out_specs=(hbm,) * 4 + (vmem,) * 8,
        scratch_shapes=[
            pltpu.VMEM((slots, width), BF16),
            pltpu.VMEM((slots, width), BF16),
            pltpu.VMEM((slots, width), BF16),
            pltpu.VMEM((loops, half + EXTRA, width), BF16),
            pltpu.VMEM((half, width), BF16),
            pltpu.VMEM((loops * half, width), BF16),
            pltpu.VMEM((2, loops * half, width), BF16),
            pltpu.VMEM((half // tq, HEADS * tq, width), BF16),
            pltpu.VMEM((half // tq, HEADS * tq, width), F32),
            pltpu.SemaphoreType.DMA((regions,)),
            pltpu.SemaphoreType.DMA((regions,)),
            pltpu.SemaphoreType.DMA((14,)),
            pltpu.SemaphoreType.DMA((14,)),
            pltpu.SemaphoreType.DMA((13,)),
        ],
        compiler_params=params(collective_id=0, has_side_effects=True),
        name="route",
    )(tokens, dest.reshape(1, rows), norm1_gain.reshape(1, width), w_qkv)
    key_rows = loops * slots + small + min(256, half)
    result = pl.pallas_call(
        functools.partial(attend_kernel, *tiles),
        out_shape=shape((slots, width), BF16),
        in_specs=[hbm] * 12 + [vmem] * 3,
        out_specs=vmem,
        scratch_shapes=[
            pltpu.VMEM((loops, half, width), BF16),
            pltpu.VMEM((slots, width), BF16),
            pltpu.VMEM((slots, width), BF16),
            pltpu.VMEM((half, width), F32),
            pltpu.VMEM((half, width), F32),
            pltpu.VMEM((width, 2 * width), BF16),
            pltpu.VMEM(w_out.shape, BF16),
            pltpu.VMEM(w_hidden.shape, BF16),
            pltpu.VMEM(w_back.shape, BF16),
            pltpu.VMEM((key_rows, width), BF16),
            pltpu.VMEM((key_rows, width), BF16),
            pltpu.VMEM((key_rows, width), BF16),
            pltpu.VMEM((HEADS * tq, width), BF16),
            pltpu.VMEM((HEADS * tq, width), F32),
            pltpu.VMEM((HEADS * tq, 128), F32),
            pltpu.VMEM((8, width), F32),
            pltpu.SemaphoreType.DMA((loops + 11,)),
        ],
        compiler_params=params(),
        name="attend",
    )(
        late, first_keys, first_a, first_b, query, raw, num, sums, w_qkv, w_out, w_hidden,
        w_back, notes, key_top, norm2_gain.reshape(1, width),
    )
    return pl.pallas_call(
        functools.partial(give_back_kernel, regions, loops),
        out_shape=jax.ShapeDtypeStruct((rows, width), BF16),
        in_specs=[vmem] * 3,
        out_specs=vmem,
        scratch_shapes=[
            pltpu.VMEM((slots, width), BF16),
            pltpu.VMEM((slots, width), BF16),
            pltpu.SemaphoreType.DMA((regions,)),
            pltpu.SemaphoreType.DMA((regions,)),
        ],
        compiler_params=params(collective_id=1, has_side_effects=True),
        name="give_back",
    )(result, rank, place)


def build(mesh, tiles):
    spread = P(("region", "loop"), None)
    return jax.shard_map(
        functools.partial(local, tiles),
        mesh=mesh,
        in_specs=(spread, spread) + (P(),) * 6,
        out_specs=spread,
        check_vma=False,
    )


def solution(mesh):
    return build(mesh, (256, 2048, 512))
```

time: 185 us -> 182 us (0.984)
  Pallas kernels: 183 us -> 180 us
    pallas_call x1, Pallas kernels: 41.5 us -> 23.1 us  [local(): pl.pallas_call(functools.partial(give_back_kernel, regions, loops), out_s...]
    pallas_call x2, Pallas kernels: 142 us -> 157 us  [the longest x1 104 us: local(): pl.pallas_call(functools.partial(attend_kernel, *tiles), out_shape=shape(...]
where the time goes in v3:
time: 182 us; the launch traced here: 181 us
  Pallas kernels  180 us (99%)
    pallas_call x1, Pallas kernels, local(): pl.pallas_call(functools.partial(attend_kernel, *tiles), out_shape=shape(...  104 us
    pallas_call x1, Pallas kernels, local(): pl.pallas_call(functools.partial(route_kernel, regions, loops, tq), out_s...  52.9 us
    pallas_call x1, Pallas kernels, local(): pl.pallas_call(functools.partial(give_back_kernel, regions, loops), out_s...  23.1 us

profile of v3, /device:TPU:1, one launch (start us, length us, event | category | flops | bytes accessed | tf_op | source)
XLA Modules:
  0.0 181.5 jit_solution(13166975476689255339)
XLA Ops:
  0.0 52.9 %route.1 = (bf16[8,512,256]{2,1,0:T(8,128)(2,1)}, bf16[4096,256]{1,0:T(8,128)(2,1)}, bf16[4096,256]{1,0:T(8,128)(2,1)}, bf16[4096,256]{1,0:T(8,128)(2,1)}, bf16[...) custom-call(bf16[512,256]{1,0:T(8,128)(2,1)} %tokens_ref.1, ...), custom_call_target="tpu_custom_call" | custom-call | tf_op jit(solution)/shard_map/route/pallas_call | solution.py:532
  52.9 103.7 %attend.1.result_ref = bf16[1024,256]{1,0:T(8,128)(2,1)} custom-call(bf16[8,512,256]{2,1,0:T(8,128)(2,1)} %get-tuple-element.17.late_hbm, bf16[4096,256]{1,0:T(8,128)(2,1)} %get-tuple-element.18.first_keys, bf16[4096,256]{1,0:T(8,128)(2,1)} %get-tuple-element.19.first_a, bf16[4096,256]{1,0:T(8,128)(2,1)} %get-tuple-element.20.first_b, ...), custom_call_target="tpu_custom_call" | custom-call | tf_op jit(solution)/shard_map/attend/pallas_call | solution.py:570
  156.7 23.1 %give_back.1 = bf16[512,256]{1,0:T(8,128)(2,1)} custom-call(bf16[1024,256]{1,0:T(8,128)(2,1)} %attend.1.result_ref, s32[8,1024]{1,0:T(8,128)} %get-tuple-element.27.rank_ref, s32[8,512]{1,0:T(8,128)} %get-tuple-element.28.place_ref), custom_call_target="tpu_custom_call" | custom-call | tf_op jit(solution)/shard_map/give_back/pallas_call | solution.py:600
  179.8 1.7 copy.10

commit v4 on v3

--- a/solution.py
+++ b/solution.py
@@ -66,7 +66,7 @@
     regions, loops, tq, tokens_ref, dest_ref, gain1_ref, wqkv_ref,
     late_ref, first_keys, first_a, first_b, query_ref, raw_ref, note_ref, num_ref, sum_ref,
     key_top, place_ref, rank_ref,
-    outbox, inbox, normed, pool, own_late, keys, vals, stacked, accum,
+    outbox, inbox, query, raw, pool, own_late, keys, vals, stacked, accum,
     send_a, recv_a, send_g, recv_g, local_sem,
 ):
     rows, width = tokens_ref.shape
@@ -93,8 +93,8 @@
 
     owner_region = dest_ref[...] // loops
     hot = one_hot(owner_region == iota((regions, rows), 0))
-    upper = one_hot(iota((rows, rows), 0) <= iota((rows, rows), 1))
-    before = jnp.dot(hot, upper, preferred_element_type=F32)
+    not_later = one_hot(iota((rows, rows), 0) <= iota((rows, rows), 1))
+    before = jnp.dot(hot, not_later, preferred_element_type=F32)
     rank = jnp.sum(before * hot.astype(F32), axis=0, keepdims=True).astype(jnp.int32) - 1
     place = owner_region * chunk + rank
     place_ref[...] = jnp.broadcast_to(place, place_ref.shape)
@@ -123,26 +123,22 @@
     inbox[own, :] = outbox[own, :]
     earlier = one_hot(iota((slots, slots), 0) < iota((slots, slots), 1))
 
-    def norm_rows(at):
-        normed[at, :] = normalize(inbox[at, :].astype(F32), gain1_ref[...]).astype(BF16)
-
-    norm_rows(own)
-    for k, copy in zip(range(1, regions), exchanges):
+    for copy in exchanges:
         copy.wait_recv()
-        source = lax.rem(region + regions - k, regions)
-        norm_rows(pl.ds(pl.multiple_of(source * chunk, chunk), chunk))
-
-    alive = jnp.where(inbox[:, :128].astype(F32) < 8.0, 1.0, 0.0)
+    landed = inbox[...]
+    normed = normalize(landed.astype(F32), gain1_ref[...]).astype(BF16)
+
+    alive = jnp.where(landed[:, :128].astype(F32) < 8.0, 1.0, 0.0)
     alive_row = alive.T[:16, :]
     ahead = jnp.dot(alive_row.astype(BF16), earlier, preferred_element_type=F32)
     slot = jnp.where(alive_row > 0.0, ahead, -1.0).astype(jnp.int32)
     rank_ref[...] = slot[:8, :]
     squeeze = one_hot(iota((slots, slots), 0) == slot[0:1, :])
-    packed = jnp.dot(squeeze, normed[...], preferred_element_type=F32).astype(BF16)
+    packed = jnp.dot(squeeze, normed, preferred_element_type=F32).astype(BF16)
     count = jnp.sum(alive_row, axis=1, keepdims=True)
-    high = jnp.floor(count * (1.0 / 128.0))
+    tens = jnp.floor(count * (1.0 / 128.0))
     pool[loop, pl.ds(0, EXTRA), :] = jnp.where(
-        iota((EXTRA, width), 1) < 128, high, count - 128.0 * high
+        iota((EXTRA, width), 1) < 128, tens, count - 128.0 * tens
     ).astype(BF16)
     pool[loop, pl.ds(EXTRA, half), :] = packed[:half, :]
     own_late[...] = packed[half:, :]
@@ -157,11 +153,15 @@
             device_id_type=MESH,
         )
 
-    def early(n, index, peer):
-        return move(n, pool.at[index], pool.at[index], peer)
-
-    def late(n, index, peer):
-        return move(n, late_ref.at[index], late_ref.at[index], peer)
+    quarter = half // 2
+    upper, lower = pl.ds(0, EXTRA + quarter), pl.ds(EXTRA + quarter, quarter)
+    high, low = pl.ds(0, quarter), pl.ds(quarter, quarter)
+
+    def early(n, index, peer, *part):
+        return move(n, pool.at[(index, *part)], pool.at[(index, *part)], peer)
+
+    def late(n, index, peer, *part):
+        return move(n, late_ref.at[(index, *part)], late_ref.at[(index, *part)], peer)
 
     moves = [
         early(0, loop, right),
@@ -170,30 +170,40 @@
         move(3, own_late, late_ref.at[loop], right),
         move(4, own_late, late_ref.at[loop], left),
         move(5, own_late, late_ref.at[loop], sibling),
-        early(6, left, right),
-        early(7, left, sibling),
-        early(8, right, sibling),
-        late(9, right, left),
-        late(10, right, sibling),
-        late(11, left, sibling),
-        early(12, far, sibling),
-        late(13, far, sibling),
+        early(6, left, right, upper),
+        early(7, right, left, lower),
+        early(8, left, sibling),
+        early(9, right, sibling),
+        early(10, far, sibling, upper),
+        early(11, far, sibling, lower),
+        late(12, left, right, high),
+        late(13, right, left, low),
+        late(14, left, sibling),
+        late(15, right, sibling),
+        late(16, far, sibling, high),
+        late(17, far, sibling, low),
     ]
-    for n in range(6):
+    for n in range(3):
         moves[n].start()
     keep = pltpu.make_async_copy(own_late, late_ref.at[loop], local_sem.at[0])
     keep.start()
 
     own_rows = jnp.concatenate([pool[loop, pl.ds(EXTRA, half), :], own_late[...]], axis=0)
     q_all = jnp.dot(own_rows, wqkv_ref[:, :width], preferred_element_type=F32).astype(BF16)
-    query_ref[...] = q_all
+    query[...] = q_all
     tiles = half // tq
     lane_head = iota((tq, width), 1) // head
     for t in range(tiles):
         q = q_all[t * tq : (t + 1) * tq, :]
         for n, h in enumerate(head_order()):
             stacked[t, n * tq : (n + 1) * tq, :] = jnp.where(lane_head == h, q, jnp.zeros_like(q))
-    raw_ref[...] = jnp.dot(squeeze, inbox[...], preferred_element_type=F32).astype(BF16)
+    raw[...] = jnp.dot(squeeze, landed, preferred_element_type=F32).astype(BF16)
+    own_out = [
+        pltpu.make_async_copy(query, query_ref, local_sem.at[13]),
+        pltpu.make_async_copy(raw, raw_ref, local_sem.at[14]),
+    ]
+    for copy in own_out:
+        copy.start()
     accum[...] = jnp.zeros_like(accum)
     key_top[...] = jnp.zeros_like(key_top)
 
@@ -233,11 +243,14 @@
             copy.start()
 
     script = {
-        0: ["w2"],
-        tiles: ["w0", "s6", "s7", "w1", "s8", "w7"],
-        tiles + tiles // 2: ["w4", "s9", "s10", "w3", "s11"],
-        2 * tiles: ["w8"],
-        3 * tiles: ["w6", "s12", "w9", "s13", "w12"],
+        0: "w2",
+        1: "w0 w1 s6 s7 s8 s9 s3 s4 s5",
+        tiles: "w8",
+        tiles + 1: "w6 w7 s10 s11",
+        2 * tiles: "w9",
+        2 * tiles + 1: "w3 w4 s12 s13 s14 s15",
+        3 * tiles: "w10 w11",
+        3 * tiles + 1: "w12 w13 s16 s17",
     }
 
     def advance(step, carry):
@@ -246,7 +259,7 @@
 
             @pl.when(step == when)
             def _(acts=acts):
-                for act in acts:
+                for act in acts.split():
                     copy = moves[int(act[1:])]
                     if act[0] == "w":
                         copy.wait_recv()
@@ -278,11 +291,12 @@
         numerator, sums = collect(accum[t], tq, width)
         num_ref[t * tq : (t + 1) * tq, :] = numerator
         sum_ref[t * tq : (t + 1) * tq, :] = sums
-    for n in (5, 10, 11, 13):
+    for n in (5, 14, 15, 16, 17):
         moves[n].wait_recv()
     for copy in exchanges + moves:
         copy.wait_send()
-    keep.wait()
+    for copy in [keep] + own_out:
+        copy.wait()
     for p in range(4):
         for copy in hand_over(p):
             copy.wait()
@@ -525,7 +539,8 @@
     half = slots // 2
     vmem = pl.BlockSpec(memory_space=pltpu.VMEM)
     hbm = pl.BlockSpec(memory_space=pltpu.HBM)
-    params = functools.partial(pltpu.CompilerParams, vmem_limit_bytes=62 * 1024 * 1024)
+    full = 62 * 1024 * 1024
+    params = pltpu.CompilerParams
     shape = jax.ShapeDtypeStruct
     (
         late, first_keys, first_a, first_b, query, raw, notes, num, sums, key_top, place, rank,
@@ -546,8 +561,9 @@
             shape((8, slots), jnp.int32),
         ),
         in_specs=[vmem] * 4,
-        out_specs=(hbm,) * 4 + (vmem,) * 8,
+        out_specs=(hbm,) * 6 + (vmem,) * 6,
         scratch_shapes=[
+            pltpu.VMEM((slots, width), BF16),
             pltpu.VMEM((slots, width), BF16),
             pltpu.VMEM((slots, width), BF16),
             pltpu.VMEM((slots, width), BF16),
@@ -559,11 +575,11 @@
             pltpu.VMEM((half // tq, HEADS * tq, width), F32),
             pltpu.SemaphoreType.DMA((regions,)),
             pltpu.SemaphoreType.DMA((regions,)),
-            pltpu.SemaphoreType.DMA((14,)),
-            pltpu.SemaphoreType.DMA((14,)),
-            pltpu.SemaphoreType.DMA((13,)),
+            pltpu.SemaphoreType.DMA((18,)),
+            pltpu.SemaphoreType.DMA((18,)),
+            pltpu.SemaphoreType.DMA((15,)),
         ],
-        compiler_params=params(collective_id=0, has_side_effects=True),
+        compiler_params=params(vmem_limit_bytes=full, collective_id=0, has_side_effects=True),
         name="route",
     )(tokens, dest.reshape(1, rows), norm1_gain.reshape(1, width), w_qkv)
     key_rows = loops * slots + small + min(256, half)
@@ -591,7 +607,7 @@
             pltpu.VMEM((8, width), F32),
             pltpu.SemaphoreType.DMA((loops + 11,)),
         ],
-        compiler_params=params(),
+        compiler_params=params(vmem_limit_bytes=full),
         name="attend",
     )(
         late, first_keys, first_a, first_b, query, raw, num, sums, w_qkv, w_out, w_hidden,
@@ -608,7 +624,7 @@
             pltpu.SemaphoreType.DMA((regions,)),
             pltpu.SemaphoreType.DMA((regions,)),
         ],
-        compiler_params=params(collective_id=1, has_side_effects=True),
+        compiler_params=params(vmem_limit_bytes=32 * 1024 * 1024, collective_id=1, has_side_effects=True),
         name="give_back",
     )(result, rank, place)
 

time: 182 us -> 186 us (1.022)
  Pallas kernels: 180 us -> 182 us
    pallas_call x1, Pallas kernels: 104 us -> 114 us  [local(): pl.pallas_call(functools.partial(attend_kernel, *tiles), out_shape=shape(...]
    pallas_call x1, Pallas kernels: 52.9 us -> 48.2 us  [local(): pl.pallas_call(functools.partial(route_kernel, regions, loops, tq), out_s...]
    pallas_call x1, Pallas kernels: 23.1 us -> 19.8 us  [local(): pl.pallas_call(functools.partial(give_back_kernel, regions, loops), out_s...]
where the time goes in v4:
time: 186 us; the launch traced here: 184 us
  Pallas kernels  182 us (98%)
    pallas_call x1, Pallas kernels, local(): pl.pallas_call(functools.partial(attend_kernel, *tiles), out_shape=shape(...  114 us
    pallas_call x1, Pallas kernels, local(): pl.pallas_call(functools.partial(route_kernel, regions, loops, tq), out_s...  48.2 us
    pallas_call x1, Pallas kernels, local(): pl.pallas_call(functools.partial(give_back_kernel, regions, loops), out_s...  19.8 us

profile of v4, /device:TPU:1, one launch (start us, length us, event | category | flops | bytes accessed | tf_op | source)
XLA Modules:
  0.0 183.9 jit_solution(2024028895584768532)
XLA Ops:
  0.0 48.2 %route.1 = (bf16[8,512,256]{2,1,0:T(8,128)(2,1)}, bf16[4096,256]{1,0:T(8,128)(2,1)}, bf16[4096,256]{1,0:T(8,128)(2,1)}, bf16[4096,256]{1,0:T(8,128)(2,1)}, bf16[...) custom-call(bf16[512,256]{1,0:T(8,128)(2,1)} %tokens_ref.1, ...), custom_call_target="tpu_custom_call" | custom-call | tf_op jit(solution)/shard_map/route/pallas_call | solution.py:547
  48.2 0.0 copy-start.1
  48.2 0.0 copy-start.2
  48.2 114.1 %attend.1.result_ref = bf16[1024,256]{1,0:T(8,128)(2,1)} custom-call(bf16[8,512,256]{2,1,0:T(8,128)(2,1)} %get-tuple-element.17.late_hbm, bf16[4096,256]{1,0:T(8,128)(2,1)} %get-tuple-element.18.first_keys, bf16[4096,256]{1,0:T(8,128)(2,1)} %get-tuple-element.19.first_a, bf16[4096,256]{1,0:T(8,128)(2,1)} %get-tuple-element.20.first_b, ...), custom_call_target="tpu_custom_call" | custom-call | tf_op jit(solution)/shard_map/attend/pallas_call | solution.py:586
  162.3 0.0 copy-done.1
  162.3 0.0 copy-done.2
  162.3 0.0 copy-start
  162.4 1.0 copy-done
  163.4 19.8 %give_back.1 = bf16[512,256]{1,0:T(8,128)(2,1)S(1)} custom-call(bf16[1024,256]{1,0:T(8,128)(2,1)S(1)} %copy-done, s32[8,1024]{1,0:T(8,128)S(1)} %copy-done.1, s32[8,512]{1,0:T(8,128)S(1)} %copy-done.2), custom_call_target="tpu_custom_call" | custom-call | tf_op jit(solution)/shard_map/give_back/pallas_call | solution.py:616
  183.2 0.7 copy.10
Async XLA Ops:
  48.2 114.1 %copy-start.1 = (s32[8,1024]{1,0:T(8,128)S(1)}, s32[8,1024]{1,0:T(8,128)}, u32[]{:S(2)}) copy-start(s32[8,1024]{1,0:T(8,128)} %get-tuple-element.27.rank_ref) | copy-start | bytes 98308
  48.2 114.1 %copy-start.2 = (s32[8,512]{1,0:T(8,128)S(1)}, s32[8,512]{1,0:T(8,128)}, u32[]{:S(2)}) copy-start(s32[8,512]{1,0:T(8,128)} %get-tuple-element.28.place_ref) | copy-start | bytes 49156
  162.3 1.0 copy-start
